TPU v7x, 256 devices: a whole 4x4x8 slice. The times are simulated.
256 devices in a mesh: sector: 64 (over x, y_hi, z), slab: 4 (over y_lo, core).
Axes of the slice: x: 4, y: 4 (y_hi: 2, y_lo: 2; y = y_hi * 2 + y_lo), z: 8, core: 2. Of those that a mesh axis runs over, the one named last changes fastest.
Arguments:
- measured: float32 [64, 262144], P('slab', 'sector'), may hold values from -64 to 64
- tof: bfloat16 [512, 16, 2, 128, 128], P('sector'), may hold values from -0.1875 to 0.1875
- tof_rows: int32 [512, 16, 2], P('sector'), may hold values from 0 to 31
- tile_owner: int32 [64], replicated, may hold values from 0 to 63, each once
Outputs:
- image: float32 [64, 131072], P('slab', 'sector')
- data_dual: float32 [64, 262144], P('slab', 'sector')
- wavelet_dual: float32 [64, 131072], P('slab', 'sector')
Inputs may be any that keep to these rules, and one draw needn't show every extreme that they name: `tile_owner`: each tile 0 to 63 is named exactly once.
All inputs are finite; a program needn't handle non-finite values.
Results may differ from a plain program's by a relative error of at most 0.0035.
Values may be sent and summed in bfloat16 or wider, within the bound.
A program may use at most 128 MiB of HBM per device.

v0:
```python
import jax
import jax.numpy as jnp
from jax import lax
from jax.sharding import PartitionSpec as P

ITERS = 3


dual_step = 0.5
primal_step = 0.15
wave_limit = 0.5
depth_limit = 0.5


def shifted(shard, axis, by):
    length = lax.axis_size(axis)
    return lax.ppermute(shard, axis, [(i, (i + by) % length) for i in range(length)])


def passed_along(block, axis, distance):
    devices = range(lax.axis_size(axis))
    route = [(i - distance, i) for i in devices if i - distance in devices]
    return lax.ppermute(block, axis, route)


def haar_pairs(upper_row, lower_row):
    sum_up = upper_row[..., 0] + upper_row[..., 1]
    dif_up = upper_row[..., 0] - upper_row[..., 1]
    sum_low = lower_row[..., 0] + lower_row[..., 1]
    dif_low = lower_row[..., 0] - lower_row[..., 1]
    top_row = jnp.stack([(sum_up + sum_low) * 0.5, (dif_up + dif_low) * 0.5], -1)
    low_row = jnp.stack([(sum_up - sum_low) * 0.5, (dif_up - dif_low) * 0.5], -1)
    return (top_row, low_row)


def body(measured, tof, tof_rows, tile_owner):
    stops = tof.shape[0]
    blocks = tof.shape[1]
    slots = tof.shape[2]
    width = tof.shape[3]
    depth_rows = measured.shape[0]
    time_blocks = measured.shape[1] // width
    pixels = blocks * width
    sectors = lax.axis_size("sector")
    band = pixels // sectors
    half = stops // 2
    flat_rows = tof_rows.reshape(-1)
    one_hot = (flat_rows[None, :] == jnp.arange(time_blocks, dtype=jnp.int32)[:, None]).astype(
        jnp.bfloat16
    )
    inverse = jnp.argsort(tile_owner)
    last_slab = lax.axis_index("slab") == lax.axis_size("slab") - 1
    row_ids = jnp.arange(depth_rows, dtype=jnp.int32)[:, None]
    keep_rows = jnp.logical_not(jnp.logical_and(last_slab, row_ids == depth_rows - 1))

    def contribute(piece, stop_at):
        shaped = piece.reshape(depth_rows, blocks, width)
        terms = jnp.einsum(
            "dbp,bkrp->dbkr", shaped, tof[stop_at], preferred_element_type=jnp.float32
        )
        return terms.reshape(depth_rows, blocks * slots, width)

    def pull(dual_half, stop_at):
        picked = dual_half.reshape(depth_rows, time_blocks, width)[:, tof_rows[stop_at]]
        gathered = jnp.einsum(
            "dbkr,bkrp->dbp", picked, tof[stop_at], preferred_element_type=jnp.float32
        )
        return gathered.reshape(depth_rows, pixels)

    def haar_tiles(tiles):
        shaped = tiles.reshape(depth_rows, sectors // 2, 2, band // 2, 2)
        top_row, low_row = haar_pairs(shaped[:, :, 0], shaped[:, :, 1])
        return jnp.stack([top_row, low_row], 2).reshape(depth_rows, pixels)

    image = jnp.zeros((depth_rows, pixels), jnp.float32)
    xbar = jnp.zeros((depth_rows, pixels), jnp.float32)
    depth_dual = jnp.zeros((depth_rows, pixels), jnp.float32)
    wavelet_dual = jnp.zeros((depth_rows, pixels), jnp.float32)
    data_dual = jnp.zeros(measured.shape, jnp.float32)
    for iteration in range(ITERS):
        forward_terms = [None] * stops
        current = shifted(xbar.astype(jnp.bfloat16), "sector", half)
        forward_terms[0] = contribute(current, 0)
        for forward_stop_at in range(1, stops):
            current = shifted(current, "sector", -1)
            forward_terms[forward_stop_at] = contribute(current, forward_stop_at)
        joined = jnp.concatenate(forward_terms, 1)
        high_part = joined.astype(jnp.bfloat16)
        low_part = (joined - high_part.astype(jnp.float32)).astype(jnp.bfloat16)
        summed = jnp.einsum("tn,dnr->dtr", one_hot, high_part, preferred_element_type=jnp.float32)
        summed = summed + jnp.einsum(
            "tn,dnr->dtr", one_hot, low_part, preferred_element_type=jnp.float32
        )
        forward_data = summed.reshape(depth_rows, time_blocks * width)
        data_dual = (data_dual + dual_step * (forward_data - measured)) / (1.0 + dual_step)
        outgoing = xbar.reshape(depth_rows, sectors, band)[:, inverse, :]
        tiles = lax.all_to_all(outgoing, "sector", split_axis=1, concat_axis=1, tiled=True).reshape(
            depth_rows, pixels
        )
        wavelet_dual = jnp.clip(
            wavelet_dual + dual_step * haar_tiles(tiles), -wave_limit, wave_limit
        )
        next_row = passed_along(xbar[:1], "slab", -1)
        diff = jnp.concatenate([xbar[1:], next_row], 0) - xbar
        depth_dual = jnp.clip(
            depth_dual + dual_step * jnp.where(keep_rows, diff, 0.0), -depth_limit, depth_limit
        )
        adjoint_dual_half = data_dual.astype(jnp.bfloat16)
        carried = pull(adjoint_dual_half, stops - 1)
        for adjoint_stop_at in range(stops - 2, -1, -1):
            carried = shifted(carried, "sector", 1) + pull(adjoint_dual_half, adjoint_stop_at)
        result = shifted(carried, "sector", -half)
        coeffs = haar_tiles(wavelet_dual).reshape(depth_rows, sectors, band)
        returned = lax.all_to_all(
            coeffs.astype(jnp.bfloat16), "sector", split_axis=1, concat_axis=1, tiled=True
        ).astype(coeffs.dtype)
        wave_back = returned[:, tile_owner, :].reshape(depth_rows, pixels)
        prev_row = passed_along(depth_dual[-1:], "slab", 1)
        update = result + wave_back + (jnp.concatenate([prev_row, depth_dual[:-1]], 0) - depth_dual)
        image_new = jnp.maximum(image - primal_step * update, 0.0)
        xbar = 2.0 * image_new - image
        image = image_new
    return (image, data_dual, wavelet_dual)


def solution(mesh):
    return jax.shard_map(
        body,
        mesh=mesh,
        in_specs=(
            P("slab", "sector"),
            P("sector", None, None, None, None),
            P("sector", None, None),
            P(),
        ),
        out_specs=(P("slab", "sector"), P("slab", "sector"), P("slab", "sector")),
        check_vma=False,
    )
```

profile of v0, /device:TPU:8, one launch (start us, length us, event | category | flops | bytes accessed | tf_op | source)
XLA Modules:
  0.0 654.0 jit_solution(3445373541841408756)
XLA Ops:
  0.6 7.3 %collective-permute-start = (bf16[16,2048]{1,0:T(8,128)(2,1)S(1)}, bf16[16,2048]{1,0:T(8,128)(2,1)S(1)}, u32[]{:S(2)}, u32[]{:S(2)}) collective-permute-start(bf16[16,2048]{1,0:T(8,128)(2,1)S(1)} %convert_element_type.67), channel_id=1, source_target_pairs={{0,16},{4,20},{8,24},{12,28},{16,32},{20,36},{24,40},{28,44},{32,4... | collective-permute-start | bytes 196616 | tf_op jit(solution)/shard_map/ppermute | solution.py:17
  13.5 8.4 %all-to-all-start = ((f32[64,1,512]{2,1,0:T(1,128)}), f32[64,1,512]{2,1,0:T(1,128)S(1)}, u32[]{:S(2)}, u32[]{:S(2)}) async-start(f32[64,1,512]{2,1,0:T(1,128)} %reshape.942), calls=%async_computation | async-start | bytes 262144 | tf_op jit(solution)/shard_map/all_to_all | solution.py:97
  33.6 7.6 %collective-permute-start.1 = (bf16[16,2048]{1,0:T(8,128)(2,1)S(1)}, bf16[16,2048]{1,0:T(8,128)(2,1)S(1)}, u32[]{:S(2)}, u32[]{:S(2)}) collective-permute-start(bf16[16,2048]{1,0:T(8,128)(2,1)S(1)} %collective-permute-done), channel_id=1, source_target_pairs={{0,252},{4,0},{8,4},{12,8},{16,12},{20,16},{24,20},{28,24},{32,28}... | collective-permute-start | bytes 196616 | tf_op jit(solution)/shard_map/ppermute | solution.py:17
  44.7 8.1 %collective-permute-start.2 = (bf16[16,2048]{1,0:T(8,128)(2,1)S(1)}, bf16[16,2048]{1,0:T(8,128)(2,1)}, u32[]{:S(2)}, u32[]{:S(2)}) collective-permute-start(bf16[16,2048]{1,0:T(8,128)(2,1)S(1)} %collective-permute-done.1), channel_id=1, source_target_pairs={{0,252},{4,0},{8,4},{12,8},{16,12},{20,16},{24,20},{28,24},{32,28}... | collective-permute-start | bytes 196616 | tf_op jit(solution)/shard_map/ppermute | solution.py:17
  57.2 8.2 %collective-permute-start.3 = (bf16[16,2048]{1,0:T(8,128)(2,1)}, bf16[16,2048]{1,0:T(8,128)(2,1)}, u32[]{:S(2)}, u32[]{:S(2)}) collective-permute-start(bf16[16,2048]{1,0:T(8,128)(2,1)} %collective-permute-done.2), channel_id=1, source_target_pairs={{0,252},{4,0},{8,4},{12,8},{16,12},{20,16},{24,20},{28,24},{32,28}... | collective-permute-start | bytes 196616 | tf_op jit(solution)/shard_map/ppermute | solution.py:17
  83.7 7.6 %collective-permute-start.4 = (bf16[16,2048]{1,0:T(8,128)(2,1)}, bf16[16,2048]{1,0:T(8,128)(2,1)S(1)}, u32[]{:S(2)}, u32[]{:S(2)}) collective-permute-start(bf16[16,2048]{1,0:T(8,128)(2,1)} %collective-permute-done.3), channel_id=1, source_target_pairs={{0,252},{4,0},{8,4},{12,8},{16,12},{20,16},{24,20},{28,24},{32,28}... | collective-permute-start | bytes 196616 | tf_op jit(solution)/shard_map/ppermute | solution.py:17
  95.2 8.3 %collective-permute-start.5 = (bf16[16,2048]{1,0:T(8,128)(2,1)S(1)}, bf16[16,2048]{1,0:T(8,128)(2,1)S(1)}, u32[]{:S(2)}, u32[]{:S(2)}) collective-permute-start(bf16[16,2048]{1,0:T(8,128)(2,1)S(1)} %collective-permute-done.4), channel_id=1, source_target_pairs={{0,252},{4,0},{8,4},{12,8},{16,12},{20,16},{24,20},{28,24},{32,28}... | collective-permute-start | bytes 196616 | tf_op jit(solution)/shard_map/ppermute | solution.py:17
  107.0 8.1 %collective-permute-start.6 = (bf16[16,2048]{1,0:T(8,128)(2,1)S(1)}, bf16[16,2048]{1,0:T(8,128)(2,1)S(1)}, u32[]{:S(2)}, u32[]{:S(2)}) collective-permute-start(bf16[16,2048]{1,0:T(8,128)(2,1)S(1)} %collective-permute-done.5), channel_id=1, source_target_pairs={{0,252},{4,0},{8,4},{12,8},{16,12},{20,16},{24,20},{28,24},{32,28}... | collective-permute-start | bytes 196616 | tf_op jit(solution)/shard_map/ppermute | solution.py:17
  118.6 8.1 %collective-permute-start.7 = (bf16[16,2048]{1,0:T(8,128)(2,1)S(1)}, bf16[16,2048]{1,0:T(8,128)(2,1)S(1)}, u32[]{:S(2)}, u32[]{:S(2)}) collective-permute-start(bf16[16,2048]{1,0:T(8,128)(2,1)S(1)} %collective-permute-done.6), channel_id=1, source_target_pairs={{0,252},{4,0},{8,4},{12,8},{16,12},{20,16},{24,20},{28,24},{32,28}... | collective-permute-start | bytes 196616 | tf_op jit(solution)/shard_map/ppermute | solution.py:17
  146.5 10.3 %collective-permute-done.9 = f32[16,2048]{1,0:T(8,128)S(1)} collective-permute-done((f32[16,2048]{1,0:T(8,128)S(1)}, f32[16,2048]{1,0:T(8,128)S(1)}, u32[]{:S(2)}, u32[]{:S(2)}) %collective-permute-start.9) | collective-permute-done | bytes 131104 | tf_op jit(solution)/shard_map/ppermute | solution.py:17
  158.4 9.5 %collective-permute-done.10 = f32[16,2048]{1,0:T(8,128)S(1)} collective-permute-done((f32[16,2048]{1,0:T(8,128)S(1)}, f32[16,2048]{1,0:T(8,128)S(1)}, u32[]{:S(2)}, u32[]{:S(2)}) %collective-permute-start.10) | collective-permute-done | bytes 131104 | tf_op jit(solution)/shard_map/ppermute | solution.py:17
  169.4 9.2 %collective-permute-done.11 = f32[16,2048]{1,0:T(8,128)S(1)} collective-permute-done((f32[16,2048]{1,0:T(8,128)S(1)}, f32[16,2048]{1,0:T(8,128)S(1)}, u32[]{:S(2)}, u32[]{:S(2)}) %collective-permute-start.11) | collective-permute-done | bytes 131104 | tf_op jit(solution)/shard_map/ppermute | solution.py:17
  180.2 9.2 %collective-permute-done.12 = f32[16,2048]{1,0:T(8,128)S(1)} collective-permute-done((f32[16,2048]{1,0:T(8,128)S(1)}, f32[16,2048]{1,0:T(8,128)S(1)}, u32[]{:S(2)}, u32[]{:S(2)}) %collective-permute-start.12) | collective-permute-done | bytes 131104 | tf_op jit(solution)/shard_map/ppermute | solution.py:17
  191.0 9.2 %collective-permute-done.13 = f32[16,2048]{1,0:T(8,128)S(1)} collective-permute-done((f32[16,2048]{1,0:T(8,128)S(1)}, f32[16,2048]{1,0:T(8,128)S(1)}, u32[]{:S(2)}, u32[]{:S(2)}) %collective-permute-start.13) | collective-permute-done | bytes 131104 | tf_op jit(solution)/shard_map/ppermute | solution.py:17
  201.8 9.2 %collective-permute-done.14 = f32[16,2048]{1,0:T(8,128)S(1)} collective-permute-done((f32[16,2048]{1,0:T(8,128)S(1)}, f32[16,2048]{1,0:T(8,128)S(1)}, u32[]{:S(2)}, u32[]{:S(2)}) %collective-permute-start.14) | collective-permute-done | bytes 131104 | tf_op jit(solution)/shard_map/ppermute | solution.py:17
  212.8 7.6 %collective-permute-done.15 = f32[16,2048]{1,0:T(8,128)S(1)} collective-permute-done((f32[16,2048]{1,0:T(8,128)S(1)}, f32[16,2048]{1,0:T(8,128)S(1)}, u32[]{:S(2)}, u32[]{:S(2)}) %collective-permute-start.15) | collective-permute-done | bytes 131104 | tf_op jit(solution)/shard_map/ppermute | solution.py:17
  225.4 6.8 %all-to-all-start.2 = ((f32[64,1,512]{2,1,0:T(1,128)}), f32[64,1,512]{2,1,0:T(1,128)S(1)}, u32[]{:S(2)}, u32[]{:S(2)}) async-start(f32[64,1,512]{2,1,0:T(1,128)} %reshape.946), calls=%async_computation.2 | async-start | bytes 262144 | tf_op jit(solution)/shard_map/all_to_all | solution.py:97
  240.4 8.3 %collective-permute-done.18 = bf16[16,2048]{1,0:T(8,128)(2,1)S(1)} collective-permute-done((bf16[16,2048]{1,0:T(8,128)(2,1)S(1)}, bf16[16,2048]{1,0:T(8,128)(2,1)S(1)}, u32[]{:S(2)}, u32[]{:S(2)}) %collective-permute-start.18) | collective-permute-done | bytes 65568 | tf_op jit(solution)/shard_map/ppermute | solution.py:17
  256.3 6.1 collective-permute-start.20
  266.7 8.2 %collective-permute-start.21 = (bf16[16,2048]{1,0:T(8,128)(2,1)}, bf16[16,2048]{1,0:T(8,128)(2,1)}, u32[]{:S(2)}, u32[]{:S(2)}) collective-permute-start(bf16[16,2048]{1,0:T(8,128)(2,1)} %collective-permute-done.20), channel_id=1, source_target_pairs={{0,252},{4,0},{8,4},{12,8},{16,12},{20,16},{24,20},{28,24},{32,28}... | collective-permute-start | bytes 196616 | tf_op jit(solution)/shard_map/ppermute | solution.py:17
  293.9 7.7 %collective-permute-start.22 = (bf16[16,2048]{1,0:T(8,128)(2,1)}, bf16[16,2048]{1,0:T(8,128)(2,1)S(1)}, u32[]{:S(2)}, u32[]{:S(2)}) collective-permute-start(bf16[16,2048]{1,0:T(8,128)(2,1)} %collective-permute-done.21), channel_id=1, source_target_pairs={{0,252},{4,0},{8,4},{12,8},{16,12},{20,16},{24,20},{28,24},{32,28}... | collective-permute-start | bytes 196616 | tf_op jit(solution)/shard_map/ppermute | solution.py:17
  305.4 8.2 %collective-permute-start.23 = (bf16[16,2048]{1,0:T(8,128)(2,1)S(1)}, bf16[16,2048]{1,0:T(8,128)(2,1)S(1)}, u32[]{:S(2)}, u32[]{:S(2)}) collective-permute-start(bf16[16,2048]{1,0:T(8,128)(2,1)S(1)} %collective-permute-done.22), channel_id=1, source_target_pairs={{0,252},{4,0},{8,4},{12,8},{16,12},{20,16},{24,20},{28,24},{32,28}... | collective-permute-start | bytes 196616 | tf_op jit(solution)/shard_map/ppermute | solution.py:17
  317.1 8.1 %collective-permute-start.24 = (bf16[16,2048]{1,0:T(8,128)(2,1)S(1)}, bf16[16,2048]{1,0:T(8,128)(2,1)S(1)}, u32[]{:S(2)}, u32[]{:S(2)}) collective-permute-start(bf16[16,2048]{1,0:T(8,128)(2,1)S(1)} %collective-permute-done.23), channel_id=1, source_target_pairs={{0,252},{4,0},{8,4},{12,8},{16,12},{20,16},{24,20},{28,24},{32,28}... | collective-permute-start | bytes 196616 | tf_op jit(solution)/shard_map/ppermute | solution.py:17
  328.7 8.1 %collective-permute-start.25 = (bf16[16,2048]{1,0:T(8,128)(2,1)S(1)}, bf16[16,2048]{1,0:T(8,128)(2,1)S(1)}, u32[]{:S(2)}, u32[]{:S(2)}) collective-permute-start(bf16[16,2048]{1,0:T(8,128)(2,1)S(1)} %collective-permute-done.24), channel_id=1, source_target_pairs={{0,252},{4,0},{8,4},{12,8},{16,12},{20,16},{24,20},{28,24},{32,28}... | collective-permute-start | bytes 196616 | tf_op jit(solution)/shard_map/ppermute | solution.py:17
  350.1 10.3 %collective-permute-done.26 = f32[16,2048]{1,0:T(8,128)S(1)} collective-permute-done((f32[16,2048]{1,0:T(8,128)S(1)}, f32[16,2048]{1,0:T(8,128)S(1)}, u32[]{:S(2)}, u32[]{:S(2)}) %collective-permute-start.26) | collective-permute-done | bytes 131104 | tf_op jit(solution)/shard_map/ppermute | solution.py:17
  362.0 10.1 %collective-permute-done.27 = f32[16,2048]{1,0:T(8,128)S(1)} collective-permute-done((f32[16,2048]{1,0:T(8,128)S(1)}, f32[16,2048]{1,0:T(8,128)S(1)}, u32[]{:S(2)}, u32[]{:S(2)}) %collective-permute-start.27) | collective-permute-done | bytes 131104 | tf_op jit(solution)/shard_map/ppermute | solution.py:17
  373.7 9.4 %collective-permute-done.28 = f32[16,2048]{1,0:T(8,128)S(1)} collective-permute-done((f32[16,2048]{1,0:T(8,128)S(1)}, f32[16,2048]{1,0:T(8,128)S(1)}, u32[]{:S(2)}, u32[]{:S(2)}) %collective-permute-start.28) | collective-permute-done | bytes 131104 | tf_op jit(solution)/shard_map/ppermute | solution.py:17
  384.6 9.2 %collective-permute-done.29 = f32[16,2048]{1,0:T(8,128)S(1)} collective-permute-done((f32[16,2048]{1,0:T(8,128)S(1)}, f32[16,2048]{1,0:T(8,128)S(1)}, u32[]{:S(2)}, u32[]{:S(2)}) %collective-permute-start.29) | collective-permute-done | bytes 131104 | tf_op jit(solution)/shard_map/ppermute | solution.py:17
  395.4 9.2 %collective-permute-done.30 = f32[16,2048]{1,0:T(8,128)S(1)} collective-permute-done((f32[16,2048]{1,0:T(8,128)S(1)}, f32[16,2048]{1,0:T(8,128)S(1)}, u32[]{:S(2)}, u32[]{:S(2)}) %collective-permute-start.30) | collective-permute-done | bytes 131104 | tf_op jit(solution)/shard_map/ppermute | solution.py:17
  406.2 9.2 %collective-permute-done.31 = f32[16,2048]{1,0:T(8,128)S(1)} collective-permute-done((f32[16,2048]{1,0:T(8,128)S(1)}, f32[16,2048]{1,0:T(8,128)S(1)}, u32[]{:S(2)}, u32[]{:S(2)}) %collective-permute-start.31) | collective-permute-done | bytes 131104 | tf_op jit(solution)/shard_map/ppermute | solution.py:17
  417.0 9.2 %collective-permute-done.32 = f32[16,2048]{1,0:T(8,128)S(1)} collective-permute-done((f32[16,2048]{1,0:T(8,128)S(1)}, f32[16,2048]{1,0:T(8,128)S(1)}, u32[]{:S(2)}, u32[]{:S(2)}) %collective-permute-start.32) | collective-permute-done | bytes 131104 | tf_op jit(solution)/shard_map/ppermute | solution.py:17
  427.8 7.6 %collective-permute-done.33 = f32[16,2048]{1,0:T(8,128)S(1)} collective-permute-done((f32[16,2048]{1,0:T(8,128)S(1)}, f32[16,2048]{1,0:T(8,128)S(1)}, u32[]{:S(2)}, u32[]{:S(2)}) %collective-permute-start.33) | collective-permute-done | bytes 131104 | tf_op jit(solution)/shard_map/ppermute | solution.py:17
  441.0 6.8 %all-to-all-start.4 = ((f32[64,1,512]{2,1,0:T(1,128)}), f32[64,1,512]{2,1,0:T(1,128)S(1)}, u32[]{:S(2)}, u32[]{:S(2)}) async-start(f32[64,1,512]{2,1,0:T(1,128)} %reshape.950), calls=%async_computation.4 | async-start | bytes 262144 | tf_op jit(solution)/shard_map/all_to_all | solution.py:97
  456.0 8.3 %collective-permute-done.36 = bf16[16,2048]{1,0:T(8,128)(2,1)S(1)} collective-permute-done((bf16[16,2048]{1,0:T(8,128)(2,1)S(1)}, bf16[16,2048]{1,0:T(8,128)(2,1)S(1)}, u32[]{:S(2)}, u32[]{:S(2)}) %collective-permute-start.36) | collective-permute-done | bytes 65568 | tf_op jit(solution)/shard_map/ppermute | solution.py:17
  471.8 6.1 collective-permute-start.38
  481.4 8.1 %collective-permute-start.39 = (bf16[16,2048]{1,0:T(8,128)(2,1)S(1)}, bf16[16,2048]{1,0:T(8,128)(2,1)S(1)}, u32[]{:S(2)}, u32[]{:S(2)}) collective-permute-start(bf16[16,2048]{1,0:T(8,128)(2,1)S(1)} %collective-permute-done.38), channel_id=1, source_target_pairs={{0,252},{4,0},{8,4},{12,8},{16,12},{20,16},{24,20},{28,24},{32,28}... | collective-permute-start | bytes 196616 | tf_op jit(solution)/shard_map/ppermute | solution.py:17
  511.0 8.1 %collective-permute-start.40 = (bf16[16,2048]{1,0:T(8,128)(2,1)S(1)}, bf16[16,2048]{1,0:T(8,128)(2,1)S(1)}, u32[]{:S(2)}, u32[]{:S(2)}) collective-permute-start(bf16[16,2048]{1,0:T(8,128)(2,1)S(1)} %collective-permute-done.39), channel_id=1, source_target_pairs={{0,252},{4,0},{8,4},{12,8},{16,12},{20,16},{24,20},{28,24},{32,28}... | collective-permute-start | bytes 196616 | tf_op jit(solution)/shard_map/ppermute | solution.py:17
  522.6 8.1 %collective-permute-start.41 = (bf16[16,2048]{1,0:T(8,128)(2,1)S(1)}, bf16[16,2048]{1,0:T(8,128)(2,1)S(1)}, u32[]{:S(2)}, u32[]{:S(2)}) collective-permute-start(bf16[16,2048]{1,0:T(8,128)(2,1)S(1)} %collective-permute-done.40), channel_id=1, source_target_pairs={{0,252},{4,0},{8,4},{12,8},{16,12},{20,16},{24,20},{28,24},{32,28}... | collective-permute-start | bytes 196616 | tf_op jit(solution)/shard_map/ppermute | solution.py:17
  534.2 8.1 %collective-permute-start.42 = (bf16[16,2048]{1,0:T(8,128)(2,1)S(1)}, bf16[16,2048]{1,0:T(8,128)(2,1)S(1)}, u32[]{:S(2)}, u32[]{:S(2)}) collective-permute-start(bf16[16,2048]{1,0:T(8,128)(2,1)S(1)} %collective-permute-done.41), channel_id=1, source_target_pairs={{0,252},{4,0},{8,4},{12,8},{16,12},{20,16},{24,20},{28,24},{32,28}... | collective-permute-start | bytes 196616 | tf_op jit(solution)/shard_map/ppermute | solution.py:17
  545.9 8.1 %collective-permute-start.43 = (bf16[16,2048]{1,0:T(8,128)(2,1)S(1)}, bf16[16,2048]{1,0:T(8,128)(2,1)S(1)}, u32[]{:S(2)}, u32[]{:S(2)}) collective-permute-start(bf16[16,2048]{1,0:T(8,128)(2,1)S(1)} %collective-permute-done.42), channel_id=1, source_target_pairs={{0,252},{4,0},{8,4},{12,8},{16,12},{20,16},{24,20},{28,24},{32,28}... | collective-permute-start | bytes 196616 | tf_op jit(solution)/shard_map/ppermute | solution.py:17
  567.4 10.3 %collective-permute-done.44 = f32[16,2048]{1,0:T(8,128)S(1)} collective-permute-done((f32[16,2048]{1,0:T(8,128)S(1)}, f32[16,2048]{1,0:T(8,128)S(1)}, u32[]{:S(2)}, u32[]{:S(2)}) %collective-permute-start.44) | collective-permute-done | bytes 131104 | tf_op jit(solution)/shard_map/ppermute | solution.py:17
  579.2 10.1 %collective-permute-done.45 = f32[16,2048]{1,0:T(8,128)S(1)} collective-permute-done((f32[16,2048]{1,0:T(8,128)S(1)}, f32[16,2048]{1,0:T(8,128)S(1)}, u32[]{:S(2)}, u32[]{:S(2)}) %collective-permute-start.45) | collective-permute-done | bytes 131104 | tf_op jit(solution)/shard_map/ppermute | solution.py:17
  591.0 9.4 %collective-permute-done.46 = f32[16,2048]{1,0:T(8,128)S(1)} collective-permute-done((f32[16,2048]{1,0:T(8,128)S(1)}, f32[16,2048]{1,0:T(8,128)S(1)}, u32[]{:S(2)}, u32[]{:S(2)}) %collective-permute-start.46) | collective-permute-done | bytes 131104 | tf_op jit(solution)/shard_map/ppermute | solution.py:17
  601.9 9.2 %collective-permute-done.47 = f32[16,2048]{1,0:T(8,128)S(1)} collective-permute-done((f32[16,2048]{1,0:T(8,128)S(1)}, f32[16,2048]{1,0:T(8,128)S(1)}, u32[]{:S(2)}, u32[]{:S(2)}) %collective-permute-start.47) | collective-permute-done | bytes 131104 | tf_op jit(solution)/shard_map/ppermute | solution.py:17
  612.7 9.2 %collective-permute-done.48 = f32[16,2048]{1,0:T(8,128)S(1)} collective-permute-done((f32[16,2048]{1,0:T(8,128)S(1)}, f32[16,2048]{1,0:T(8,128)S(1)}, u32[]{:S(2)}, u32[]{:S(2)}) %collective-permute-start.48) | collective-permute-done | bytes 131104 | tf_op jit(solution)/shard_map/ppermute | solution.py:17
  623.5 9.2 %collective-permute-done.49 = f32[16,2048]{1,0:T(8,128)S(1)} collective-permute-done((f32[16,2048]{1,0:T(8,128)S(1)}, f32[16,2048]{1,0:T(8,128)S(1)}, u32[]{:S(2)}, u32[]{:S(2)}) %collective-permute-start.49) | collective-permute-done | bytes 131104 | tf_op jit(solution)/shard_map/ppermute | solution.py:17
  634.3 9.2 %collective-permute-done.50 = f32[16,2048]{1,0:T(8,128)S(1)} collective-permute-done((f32[16,2048]{1,0:T(8,128)S(1)}, f32[16,2048]{1,0:T(8,128)S(1)}, u32[]{:S(2)}, u32[]{:S(2)}) %collective-permute-start.50) | collective-permute-done | bytes 131104 | tf_op jit(solution)/shard_map/ppermute | solution.py:17
  644.8 7.6 %collective-permute-done.51 = f32[16,2048]{1,0:T(8,128)S(1)} collective-permute-done((f32[16,2048]{1,0:T(8,128)S(1)}, f32[16,2048]{1,0:T(8,128)S(1)}, u32[]{:S(2)}, u32[]{:S(2)}) %collective-permute-start.51) | collective-permute-done | bytes 131104 | tf_op jit(solution)/shard_map/ppermute | solution.py:17
  (421 shorter events, 243.8 us)
Async XLA Ops:
  0.6 31.3 %collective-permute-start = (bf16[16,2048]{1,0:T(8,128)(2,1)S(1)}, bf16[16,2048]{1,0:T(8,128)(2,1)S(1)}, u32[]{:S(2)}, u32[]{:S(2)}) collective-permute-start(bf16[16,2048]{1,0:T(8,128)(2,1)S(1)} %convert_element_type.67), channel_id=1, source_target_pairs={{0,16},{4,20},{8,24},{12,28},{16,32},{20,36},{24,40},{28,44},{32,4... | collective-permute-start | bytes 196616 | tf_op jit(solution)/shard_map/ppermute | solution.py:17
  13.5 52.0 %all-to-all-start = ((f32[64,1,512]{2,1,0:T(1,128)}), f32[64,1,512]{2,1,0:T(1,128)S(1)}, u32[]{:S(2)}, u32[]{:S(2)}) async-start(f32[64,1,512]{2,1,0:T(1,128)} %reshape.942), calls=%async_computation | async-start | bytes 262144 | tf_op jit(solution)/shard_map/all_to_all | solution.py:97
  29.8 183.0 %collective-permute-start.17 = (f32[1,2048]{1,0:T(1,128)}, f32[1,2048]{1,0:T(1,128)}, u32[]{:S(2)}, u32[]{:S(2)}) collective-permute-start(f32[1,2048]{1,0:T(1,128)} %slice.405), channel_id=1, source_target_pairs={{0,1},{1,2},{2,3},{4,5},{5,6},{6,7},{8,9},{9,10},{10,11},{12,13},{... | collective-permute-start | bytes 24584 | tf_op jit(solution)/shard_map/ppermute | solution.py:23
  44.7 10.0 %collective-permute-start.2 = (bf16[16,2048]{1,0:T(8,128)(2,1)S(1)}, bf16[16,2048]{1,0:T(8,128)(2,1)}, u32[]{:S(2)}, u32[]{:S(2)}) collective-permute-start(bf16[16,2048]{1,0:T(8,128)(2,1)S(1)} %collective-permute-done.1), channel_id=1, source_target_pairs={{0,252},{4,0},{8,4},{12,8},{16,12},{20,16},{24,20},{28,24},{32,28}... | collective-permute-start | bytes 196616 | tf_op jit(solution)/shard_map/ppermute | solution.py:17
  57.2 24.1 %collective-permute-start.3 = (bf16[16,2048]{1,0:T(8,128)(2,1)}, bf16[16,2048]{1,0:T(8,128)(2,1)}, u32[]{:S(2)}, u32[]{:S(2)}) collective-permute-start(bf16[16,2048]{1,0:T(8,128)(2,1)} %collective-permute-done.2), channel_id=1, source_target_pairs={{0,252},{4,0},{8,4},{12,8},{16,12},{20,16},{24,20},{28,24},{32,28}... | collective-permute-start | bytes 196616 | tf_op jit(solution)/shard_map/ppermute | solution.py:17
  76.6 26.9 %all-to-all-start.1 = ((bf16[64,2,256]{2,1,0:T(2,128)(2,1)}), bf16[64,2,256]{2,1,0:T(2,128)(2,1)S(1)}, u32[]{:S(2)}, u32[]{:S(2)}) async-start(bf16[64,2,256]{2,1,0:T(2,128)(2,1)} %reshape.944), calls=%async_computation.1 | async-start | bytes 131072 | tf_op jit(solution)/shard_map/all_to_all | solution.py:114
  95.2 10.2 %collective-permute-start.5 = (bf16[16,2048]{1,0:T(8,128)(2,1)S(1)}, bf16[16,2048]{1,0:T(8,128)(2,1)S(1)}, u32[]{:S(2)}, u32[]{:S(2)}) collective-permute-start(bf16[16,2048]{1,0:T(8,128)(2,1)S(1)} %collective-permute-done.4), channel_id=1, source_target_pairs={{0,252},{4,0},{8,4},{12,8},{16,12},{20,16},{24,20},{28,24},{32,28}... | collective-permute-start | bytes 196616 | tf_op jit(solution)/shard_map/ppermute | solution.py:17
  107.0 10.0 %collective-permute-start.6 = (bf16[16,2048]{1,0:T(8,128)(2,1)S(1)}, bf16[16,2048]{1,0:T(8,128)(2,1)S(1)}, u32[]{:S(2)}, u32[]{:S(2)}) collective-permute-start(bf16[16,2048]{1,0:T(8,128)(2,1)S(1)} %collective-permute-done.5), channel_id=1, source_target_pairs={{0,252},{4,0},{8,4},{12,8},{16,12},{20,16},{24,20},{28,24},{32,28}... | collective-permute-start | bytes 196616 | tf_op jit(solution)/shard_map/ppermute | solution.py:17
  118.6 10.0 %collective-permute-start.7 = (bf16[16,2048]{1,0:T(8,128)(2,1)S(1)}, bf16[16,2048]{1,0:T(8,128)(2,1)S(1)}, u32[]{:S(2)}, u32[]{:S(2)}) collective-permute-start(bf16[16,2048]{1,0:T(8,128)(2,1)S(1)} %collective-permute-done.6), channel_id=1, source_target_pairs={{0,252},{4,0},{8,4},{12,8},{16,12},{20,16},{24,20},{28,24},{32,28}... | collective-permute-start | bytes 196616 | tf_op jit(solution)/shard_map/ppermute | solution.py:17
  133.2 11.7 %collective-permute-start.8 = (f32[16,2048]{1,0:T(8,128)S(1)}, f32[16,2048]{1,0:T(8,128)S(1)}, u32[]{:S(2)}, u32[]{:S(2)}) collective-permute-start(f32[16,2048]{1,0:T(8,128)S(1)} %bitcast.854), channel_id=1, source_target_pairs={{0,4},{4,8},{8,12},{12,16},{16,20},{20,24},{24,28},{28,32},{32,36}... | collective-permute-start | bytes 393224 | tf_op jit(solution)/shard_map/ppermute | solution.py:17
  144.9 11.9 %collective-permute-start.9 = (f32[16,2048]{1,0:T(8,128)S(1)}, f32[16,2048]{1,0:T(8,128)S(1)}, u32[]{:S(2)}, u32[]{:S(2)}) collective-permute-start(f32[16,2048]{1,0:T(8,128)S(1)} %bitcast_add_fusion.20), channel_id=1, source_target_pairs={{0,4},{4,8},{8,12},{12,16},{16,20},{20,24},{24,28},{28,32},{32,36}... | collective-permute-start | bytes 393224 | tf_op jit(solution)/shard_map/ppermute | solution.py:17
  156.8 11.0 %collective-permute-start.10 = (f32[16,2048]{1,0:T(8,128)S(1)}, f32[16,2048]{1,0:T(8,128)S(1)}, u32[]{:S(2)}, u32[]{:S(2)}) collective-permute-start(f32[16,2048]{1,0:T(8,128)S(1)} %bitcast_add_fusion.19), channel_id=1, source_target_pairs={{0,4},{4,8},{8,12},{12,16},{16,20},{20,24},{24,28},{28,32},{32,36}... | collective-permute-start | bytes 393224 | tf_op jit(solution)/shard_map/ppermute | solution.py:17
  167.9 10.8 %collective-permute-start.11 = (f32[16,2048]{1,0:T(8,128)S(1)}, f32[16,2048]{1,0:T(8,128)S(1)}, u32[]{:S(2)}, u32[]{:S(2)}) collective-permute-start(f32[16,2048]{1,0:T(8,128)S(1)} %bitcast_add_fusion.18), channel_id=1, source_target_pairs={{0,4},{4,8},{8,12},{12,16},{16,20},{20,24},{24,28},{28,32},{32,36}... | collective-permute-start | bytes 393224 | tf_op jit(solution)/shard_map/ppermute | solution.py:17
  178.6 10.8 %collective-permute-start.12 = (f32[16,2048]{1,0:T(8,128)S(1)}, f32[16,2048]{1,0:T(8,128)S(1)}, u32[]{:S(2)}, u32[]{:S(2)}) collective-permute-start(f32[16,2048]{1,0:T(8,128)S(1)} %bitcast_add_fusion.17), channel_id=1, source_target_pairs={{0,4},{4,8},{8,12},{12,16},{16,20},{20,24},{24,28},{28,32},{32,36}... | collective-permute-start | bytes 393224 | tf_op jit(solution)/shard_map/ppermute | solution.py:17
  189.4 10.8 %collective-permute-start.13 = (f32[16,2048]{1,0:T(8,128)S(1)}, f32[16,2048]{1,0:T(8,128)S(1)}, u32[]{:S(2)}, u32[]{:S(2)}) collective-permute-start(f32[16,2048]{1,0:T(8,128)S(1)} %bitcast_add_fusion.16), channel_id=1, source_target_pairs={{0,4},{4,8},{8,12},{12,16},{16,20},{20,24},{24,28},{28,32},{32,36}... | collective-permute-start | bytes 393224 | tf_op jit(solution)/shard_map/ppermute | solution.py:17
  200.2 10.8 %collective-permute-start.14 = (f32[16,2048]{1,0:T(8,128)S(1)}, f32[16,2048]{1,0:T(8,128)S(1)}, u32[]{:S(2)}, u32[]{:S(2)}) collective-permute-start(f32[16,2048]{1,0:T(8,128)S(1)} %bitcast_add_fusion.15), channel_id=1, source_target_pairs={{0,4},{4,8},{8,12},{12,16},{16,20},{20,24},{24,28},{28,32},{32,36}... | collective-permute-start | bytes 393224 | tf_op jit(solution)/shard_map/ppermute | solution.py:17
  222.5 15.3 %collective-permute-start.34 = (f32[1,2048]{1,0:T(1,128)S(1)}, f32[1,2048]{1,0:T(1,128)S(1)}, u32[]{:S(2)}, u32[]{:S(2)}) collective-permute-start(f32[1,2048]{1,0:T(1,128)S(1)} %slice.420), channel_id=1, source_target_pairs={{1,0},{2,1},{3,2},{5,4},{6,5},{7,6},{9,8},{10,9},{11,10},{13,12},{... | collective-permute-start | bytes 24584 | tf_op jit(solution)/shard_map/ppermute | solution.py:23
  225.4 49.6 %all-to-all-start.2 = ((f32[64,1,512]{2,1,0:T(1,128)}), f32[64,1,512]{2,1,0:T(1,128)S(1)}, u32[]{:S(2)}, u32[]{:S(2)}) async-start(f32[64,1,512]{2,1,0:T(1,128)} %reshape.946), calls=%async_computation.2 | async-start | bytes 262144 | tf_op jit(solution)/shard_map/all_to_all | solution.py:97
  232.2 16.5 %collective-permute-start.18 = (bf16[16,2048]{1,0:T(8,128)(2,1)S(1)}, bf16[16,2048]{1,0:T(8,128)(2,1)S(1)}, u32[]{:S(2)}, u32[]{:S(2)}) collective-permute-start(bf16[16,2048]{1,0:T(8,128)(2,1)S(1)} %get-tuple-element.19), channel_id=1, source_target_pairs={{0,16},{4,20},{8,24},{12,28},{16,32},{20,36},{24,40},{28,44},{32,4... | collective-permute-start | bytes 196616 | tf_op jit(solution)/shard_map/ppermute | solution.py:17
  238.5 189.3 %collective-permute-start.35 = (f32[1,2048]{1,0:T(1,128)}, f32[1,2048]{1,0:T(1,128)}, u32[]{:S(2)}, u32[]{:S(2)}) collective-permute-start(f32[1,2048]{1,0:T(1,128)} %slice.421), channel_id=1, source_target_pairs={{0,1},{1,2},{2,3},{4,5},{5,6},{6,7},{8,9},{9,10},{10,11},{12,13},{... | collective-permute-start | bytes 24584 | tf_op jit(solution)/shard_map/ppermute | solution.py:23
  266.7 24.7 %collective-permute-start.21 = (bf16[16,2048]{1,0:T(8,128)(2,1)}, bf16[16,2048]{1,0:T(8,128)(2,1)}, u32[]{:S(2)}, u32[]{:S(2)}) collective-permute-start(bf16[16,2048]{1,0:T(8,128)(2,1)} %collective-permute-done.20), channel_id=1, source_target_pairs={{0,252},{4,0},{8,4},{12,8},{16,12},{20,16},{24,20},{28,24},{32,28}... | collective-permute-start | bytes 196616 | tf_op jit(solution)/shard_map/ppermute | solution.py:17
  286.6 27.0 %all-to-all-start.3 = ((bf16[64,2,256]{2,1,0:T(2,128)(2,1)}), bf16[64,2,256]{2,1,0:T(2,128)(2,1)S(1)}, u32[]{:S(2)}, u32[]{:S(2)}) async-start(bf16[64,2,256]{2,1,0:T(2,128)(2,1)} %reshape.948), calls=%async_computation.3 | async-start | bytes 131072 | tf_op jit(solution)/shard_map/all_to_all | solution.py:114
  305.4 10.1 %collective-permute-start.23 = (bf16[16,2048]{1,0:T(8,128)(2,1)S(1)}, bf16[16,2048]{1,0:T(8,128)(2,1)S(1)}, u32[]{:S(2)}, u32[]{:S(2)}) collective-permute-start(bf16[16,2048]{1,0:T(8,128)(2,1)S(1)} %collective-permute-done.22), channel_id=1, source_target_pairs={{0,252},{4,0},{8,4},{12,8},{16,12},{20,16},{24,20},{28,24},{32,28}... | collective-permute-start | bytes 196616 | tf_op jit(solution)/shard_map/ppermute | solution.py:17
  317.1 10.0 %collective-permute-start.24 = (bf16[16,2048]{1,0:T(8,128)(2,1)S(1)}, bf16[16,2048]{1,0:T(8,128)(2,1)S(1)}, u32[]{:S(2)}, u32[]{:S(2)}) collective-permute-start(bf16[16,2048]{1,0:T(8,128)(2,1)S(1)} %collective-permute-done.23), channel_id=1, source_target_pairs={{0,252},{4,0},{8,4},{12,8},{16,12},{20,16},{24,20},{28,24},{32,28}... | collective-permute-start | bytes 196616 | tf_op jit(solution)/shard_map/ppermute | solution.py:17
  328.7 10.0 %collective-permute-start.25 = (bf16[16,2048]{1,0:T(8,128)(2,1)S(1)}, bf16[16,2048]{1,0:T(8,128)(2,1)S(1)}, u32[]{:S(2)}, u32[]{:S(2)}) collective-permute-start(bf16[16,2048]{1,0:T(8,128)(2,1)S(1)} %collective-permute-done.24), channel_id=1, source_target_pairs={{0,252},{4,0},{8,4},{12,8},{16,12},{20,16},{24,20},{28,24},{32,28}... | collective-permute-start | bytes 196616 | tf_op jit(solution)/shard_map/ppermute | solution.py:17
  348.6 11.8 %collective-permute-start.26 = (f32[16,2048]{1,0:T(8,128)S(1)}, f32[16,2048]{1,0:T(8,128)S(1)}, u32[]{:S(2)}, u32[]{:S(2)}) collective-permute-start(f32[16,2048]{1,0:T(8,128)S(1)} %bitcast.855), channel_id=1, source_target_pairs={{0,4},{4,8},{8,12},{12,16},{16,20},{20,24},{24,28},{28,32},{32,36}... | collective-permute-start | bytes 393224 | tf_op jit(solution)/shard_map/ppermute | solution.py:17
  360.4 11.7 %collective-permute-start.27 = (f32[16,2048]{1,0:T(8,128)S(1)}, f32[16,2048]{1,0:T(8,128)S(1)}, u32[]{:S(2)}, u32[]{:S(2)}) collective-permute-start(f32[16,2048]{1,0:T(8,128)S(1)} %bitcast_add_fusion.13), channel_id=1, source_target_pairs={{0,4},{4,8},{8,12},{12,16},{16,20},{20,24},{24,28},{28,32},{32,36}... | collective-permute-start | bytes 393224 | tf_op jit(solution)/shard_map/ppermute | solution.py:17
  372.1 10.9 %collective-permute-start.28 = (f32[16,2048]{1,0:T(8,128)S(1)}, f32[16,2048]{1,0:T(8,128)S(1)}, u32[]{:S(2)}, u32[]{:S(2)}) collective-permute-start(f32[16,2048]{1,0:T(8,128)S(1)} %bitcast_add_fusion.12), channel_id=1, source_target_pairs={{0,4},{4,8},{8,12},{12,16},{16,20},{20,24},{24,28},{28,32},{32,36}... | collective-permute-start | bytes 393224 | tf_op jit(solution)/shard_map/ppermute | solution.py:17
  383.1 10.8 %collective-permute-start.29 = (f32[16,2048]{1,0:T(8,128)S(1)}, f32[16,2048]{1,0:T(8,128)S(1)}, u32[]{:S(2)}, u32[]{:S(2)}) collective-permute-start(f32[16,2048]{1,0:T(8,128)S(1)} %bitcast_add_fusion.11), channel_id=1, source_target_pairs={{0,4},{4,8},{8,12},{12,16},{16,20},{20,24},{24,28},{28,32},{32,36}... | collective-permute-start | bytes 393224 | tf_op jit(solution)/shard_map/ppermute | solution.py:17
  393.9 10.8 %collective-permute-start.30 = (f32[16,2048]{1,0:T(8,128)S(1)}, f32[16,2048]{1,0:T(8,128)S(1)}, u32[]{:S(2)}, u32[]{:S(2)}) collective-permute-start(f32[16,2048]{1,0:T(8,128)S(1)} %bitcast_add_fusion.10), channel_id=1, source_target_pairs={{0,4},{4,8},{8,12},{12,16},{16,20},{20,24},{24,28},{28,32},{32,36}... | collective-permute-start | bytes 393224 | tf_op jit(solution)/shard_map/ppermute | solution.py:17
  404.6 10.8 %collective-permute-start.31 = (f32[16,2048]{1,0:T(8,128)S(1)}, f32[16,2048]{1,0:T(8,128)S(1)}, u32[]{:S(2)}, u32[]{:S(2)}) collective-permute-start(f32[16,2048]{1,0:T(8,128)S(1)} %bitcast_add_fusion.9), channel_id=1, source_target_pairs={{0,4},{4,8},{8,12},{12,16},{16,20},{20,24},{24,28},{28,32},{32,36}... | collective-permute-start | bytes 393224 | tf_op jit(solution)/shard_map/ppermute | solution.py:17
  415.4 10.8 %collective-permute-start.32 = (f32[16,2048]{1,0:T(8,128)S(1)}, f32[16,2048]{1,0:T(8,128)S(1)}, u32[]{:S(2)}, u32[]{:S(2)}) collective-permute-start(f32[16,2048]{1,0:T(8,128)S(1)} %bitcast_add_fusion.8), channel_id=1, source_target_pairs={{0,4},{4,8},{8,12},{12,16},{16,20},{20,24},{24,28},{28,32},{32,36}... | collective-permute-start | bytes 393224 | tf_op jit(solution)/shard_map/ppermute | solution.py:17
  438.0 15.3 %collective-permute-start.52 = (f32[1,2048]{1,0:T(1,128)S(1)}, f32[1,2048]{1,0:T(1,128)S(1)}, u32[]{:S(2)}, u32[]{:S(2)}) collective-permute-start(f32[1,2048]{1,0:T(1,128)S(1)} %slice.436), channel_id=1, source_target_pairs={{1,0},{2,1},{3,2},{5,4},{6,5},{7,6},{9,8},{10,9},{11,10},{13,12},{... | collective-permute-start | bytes 24584 | tf_op jit(solution)/shard_map/ppermute | solution.py:23
  441.0 48.6 %all-to-all-start.4 = ((f32[64,1,512]{2,1,0:T(1,128)}), f32[64,1,512]{2,1,0:T(1,128)S(1)}, u32[]{:S(2)}, u32[]{:S(2)}) async-start(f32[64,1,512]{2,1,0:T(1,128)} %reshape.950), calls=%async_computation.4 | async-start | bytes 262144 | tf_op jit(solution)/shard_map/all_to_all | solution.py:97
  447.8 16.5 %collective-permute-start.36 = (bf16[16,2048]{1,0:T(8,128)(2,1)S(1)}, bf16[16,2048]{1,0:T(8,128)(2,1)S(1)}, u32[]{:S(2)}, u32[]{:S(2)}) collective-permute-start(bf16[16,2048]{1,0:T(8,128)(2,1)S(1)} %get-tuple-element.16), channel_id=1, source_target_pairs={{0,16},{4,20},{8,24},{12,28},{16,32},{20,36},{24,40},{28,44},{32,4... | collective-permute-start | bytes 196616 | tf_op jit(solution)/shard_map/ppermute | solution.py:17
  454.0 190.8 %collective-permute-start.53 = (f32[1,2048]{1,0:T(1,128)}, f32[1,2048]{1,0:T(1,128)}, u32[]{:S(2)}, u32[]{:S(2)}) collective-permute-start(f32[1,2048]{1,0:T(1,128)} %slice.437), channel_id=1, source_target_pairs={{0,1},{1,2},{2,3},{4,5},{5,6},{6,7},{8,9},{9,10},{10,11},{12,13},{... | collective-permute-start | bytes 24584 | tf_op jit(solution)/shard_map/ppermute | solution.py:23
  481.4 28.0 %collective-permute-start.39 = (bf16[16,2048]{1,0:T(8,128)(2,1)S(1)}, bf16[16,2048]{1,0:T(8,128)(2,1)S(1)}, u32[]{:S(2)}, u32[]{:S(2)}) collective-permute-start(bf16[16,2048]{1,0:T(8,128)(2,1)S(1)} %collective-permute-done.38), channel_id=1, source_target_pairs={{0,252},{4,0},{8,4},{12,8},{16,12},{20,16},{24,20},{28,24},{32,28}... | collective-permute-start | bytes 196616 | tf_op jit(solution)/shard_map/ppermute | solution.py:17
  502.4 28.4 %all-to-all-start.5 = ((bf16[64,2,256]{2,1,0:T(2,128)(2,1)}), bf16[64,2,256]{2,1,0:T(2,128)(2,1)S(1)}, u32[]{:S(2)}, u32[]{:S(2)}) async-start(bf16[64,2,256]{2,1,0:T(2,128)(2,1)} %reshape.952), calls=%async_computation.5 | async-start | bytes 131072 | tf_op jit(solution)/shard_map/all_to_all | solution.py:114
  522.6 10.0 %collective-permute-start.41 = (bf16[16,2048]{1,0:T(8,128)(2,1)S(1)}, bf16[16,2048]{1,0:T(8,128)(2,1)S(1)}, u32[]{:S(2)}, u32[]{:S(2)}) collective-permute-start(bf16[16,2048]{1,0:T(8,128)(2,1)S(1)} %collective-permute-done.40), channel_id=1, source_target_pairs={{0,252},{4,0},{8,4},{12,8},{16,12},{20,16},{24,20},{28,24},{32,28}... | collective-permute-start | bytes 196616 | tf_op jit(solution)/shard_map/ppermute | solution.py:17
  534.2 10.0 %collective-permute-start.42 = (bf16[16,2048]{1,0:T(8,128)(2,1)S(1)}, bf16[16,2048]{1,0:T(8,128)(2,1)S(1)}, u32[]{:S(2)}, u32[]{:S(2)}) collective-permute-start(bf16[16,2048]{1,0:T(8,128)(2,1)S(1)} %collective-permute-done.41), channel_id=1, source_target_pairs={{0,252},{4,0},{8,4},{12,8},{16,12},{20,16},{24,20},{28,24},{32,28}... | collective-permute-start | bytes 196616 | tf_op jit(solution)/shard_map/ppermute | solution.py:17
  545.9 10.0 %collective-permute-start.43 = (bf16[16,2048]{1,0:T(8,128)(2,1)S(1)}, bf16[16,2048]{1,0:T(8,128)(2,1)S(1)}, u32[]{:S(2)}, u32[]{:S(2)}) collective-permute-start(bf16[16,2048]{1,0:T(8,128)(2,1)S(1)} %collective-permute-done.42), channel_id=1, source_target_pairs={{0,252},{4,0},{8,4},{12,8},{16,12},{20,16},{24,20},{28,24},{32,28}... | collective-permute-start | bytes 196616 | tf_op jit(solution)/shard_map/ppermute | solution.py:17
  565.8 11.8 %collective-permute-start.44 = (f32[16,2048]{1,0:T(8,128)S(1)}, f32[16,2048]{1,0:T(8,128)S(1)}, u32[]{:S(2)}, u32[]{:S(2)}) collective-permute-start(f32[16,2048]{1,0:T(8,128)S(1)} %bitcast.856), channel_id=1, source_target_pairs={{0,4},{4,8},{8,12},{12,16},{16,20},{20,24},{24,28},{28,32},{32,36}... | collective-permute-start | bytes 393224 | tf_op jit(solution)/shard_map/ppermute | solution.py:17
  577.7 11.7 %collective-permute-start.45 = (f32[16,2048]{1,0:T(8,128)S(1)}, f32[16,2048]{1,0:T(8,128)S(1)}, u32[]{:S(2)}, u32[]{:S(2)}) collective-permute-start(f32[16,2048]{1,0:T(8,128)S(1)} %bitcast_add_fusion.6), channel_id=1, source_target_pairs={{0,4},{4,8},{8,12},{12,16},{16,20},{20,24},{24,28},{28,32},{32,36}... | collective-permute-start | bytes 393224 | tf_op jit(solution)/shard_map/ppermute | solution.py:17
  589.4 10.9 %collective-permute-start.46 = (f32[16,2048]{1,0:T(8,128)S(1)}, f32[16,2048]{1,0:T(8,128)S(1)}, u32[]{:S(2)}, u32[]{:S(2)}) collective-permute-start(f32[16,2048]{1,0:T(8,128)S(1)} %bitcast_add_fusion.5), channel_id=1, source_target_pairs={{0,4},{4,8},{8,12},{12,16},{16,20},{20,24},{24,28},{28,32},{32,36}... | collective-permute-start | bytes 393224 | tf_op jit(solution)/shard_map/ppermute | solution.py:17
  600.3 10.8 %collective-permute-start.47 = (f32[16,2048]{1,0:T(8,128)S(1)}, f32[16,2048]{1,0:T(8,128)S(1)}, u32[]{:S(2)}, u32[]{:S(2)}) collective-permute-start(f32[16,2048]{1,0:T(8,128)S(1)} %bitcast_add_fusion.4), channel_id=1, source_target_pairs={{0,4},{4,8},{8,12},{12,16},{16,20},{20,24},{24,28},{28,32},{32,36}... | collective-permute-start | bytes 393224 | tf_op jit(solution)/shard_map/ppermute | solution.py:17
  611.1 10.8 %collective-permute-start.48 = (f32[16,2048]{1,0:T(8,128)S(1)}, f32[16,2048]{1,0:T(8,128)S(1)}, u32[]{:S(2)}, u32[]{:S(2)}) collective-permute-start(f32[16,2048]{1,0:T(8,128)S(1)} %bitcast_add_fusion.3), channel_id=1, source_target_pairs={{0,4},{4,8},{8,12},{12,16},{16,20},{20,24},{24,28},{28,32},{32,36}... | collective-permute-start | bytes 393224 | tf_op jit(solution)/shard_map/ppermute | solution.py:17
  621.9 10.8 %collective-permute-start.49 = (f32[16,2048]{1,0:T(8,128)S(1)}, f32[16,2048]{1,0:T(8,128)S(1)}, u32[]{:S(2)}, u32[]{:S(2)}) collective-permute-start(f32[16,2048]{1,0:T(8,128)S(1)} %bitcast_add_fusion.2), channel_id=1, source_target_pairs={{0,4},{4,8},{8,12},{12,16},{16,20},{20,24},{24,28},{28,32},{32,36}... | collective-permute-start | bytes 393224 | tf_op jit(solution)/shard_map/ppermute | solution.py:17
  632.7 10.8 %collective-permute-start.50 = (f32[16,2048]{1,0:T(8,128)S(1)}, f32[16,2048]{1,0:T(8,128)S(1)}, u32[]{:S(2)}, u32[]{:S(2)}) collective-permute-start(f32[16,2048]{1,0:T(8,128)S(1)} %bitcast_add_fusion.1), channel_id=1, source_target_pairs={{0,4},{4,8},{8,12},{12,16},{16,20},{20,24},{24,28},{28,32},{32,36}... | collective-permute-start | bytes 393224 | tf_op jit(solution)/shard_map/ppermute | solution.py:17
  (44 other events, 1544.6 us)
where the time goes:
time: 666 us; the launch traced here: 654 us
  waiting for transfers between devices  272 us (41%)
  starting transfers between devices  219 us (33%)
  matrix products  75.3 us (11%)
  local copies, waits for them, and re-layouts  66.8 us (10%)
  other arithmetic  18.5 us (3%)
    ppermute x48, waiting for transfers between devices, shifted(): lax.ppermute(shard, axis, [(i, (i + by) % length) for i in range(length)])  272 us
    ppermute x48, starting transfers between devices, shifted(): lax.ppermute(shard, axis, [(i, (i + by) % length) for i in range(length)])  171 us
    dot_general x24, matrix products, contribute(): jnp.einsum('dbp,bkrp->dbkr', shaped, tof[stop_at], preferred_element_type...  38.4 us
    dot_general x24, matrix products, pull(): jnp.einsum('dbkr,bkrp->dbp', picked, tof[stop_at], preferred_element_type...  35.3 us
    unnamed x132, local copies, waits for them, and re-layouts  27.7 us
    all_to_all x3, starting transfers between devices, body(): lax.all_to_all(outgoing, 'sector', split_axis=1, concat_axis=1, tiled=True)  22 us
    gather x24, local copies, waits for them, and re-layouts, pull(): dual_half.reshape(depth_rows, time_blocks, width)[:, tof_rows[stop_at]]  14.6 us
    all_to_all x3, starting transfers between devices, body(): lax.all_to_all(coeffs.astype(jnp.bfloat16), 'sector', split_axis=1, conca...  14.1 us
  transfers between devices with their start and end apart: 60, of which 44 were waited for; matrix products, arithmetic and copies ran while one was open for 23% of the time, Pallas kernels for 0%

commit v1 on v0

v1 whole, which is shorter than its diff:
```python
import functools

import jax
import jax.numpy as jnp
from jax import lax
from jax.experimental import pallas as pl
from jax.experimental.pallas import tpu as pltpu
from jax.sharding import PartitionSpec as P

ITERS = 3
STOPS = 8
HALF = STOPS // 2
ZS = 8

dual_step = 0.5
primal_step = 0.15
wave_limit = 0.5
depth_limit = 0.5


def far_first(i):
    return (i % 2) * (STOPS - 1) + (1 - 2 * (i % 2)) * (i // 2)


def near_first(i):
    return far_first(6 - i)


def kernel(
    sectors, groups, slabs, blocks, time_blocks,
    rows_ref, prev_ref, owner_ref, inverse_ref, measured_ref, tof_hbm,
    image_ref, data_ref, wave_ref,
    tof, sums, dual_half, xbar, depth, halo, total,
    shares, partials_out, partials_in, edge_out, edge_in,
    rolled, bands, mid, tiles, wave, rolled_back, back_bands, wave_back,
    load_sem, share_send, share_recv, part_send, part_recv, edge_send, edge_recv,
    band_send, band_recv,
):
    me = lax.axis_index("sector")
    slab = lax.axis_index("slab")
    group, zed = me // ZS, lax.rem(me, ZS)
    terms = STOPS * blocks * 2

    loads = [
        pltpu.make_async_copy(tof_hbm.at[j], tof.at[j], load_sem.at[j]) for j in range(STOPS)
    ]
    for i in (0, 7, 1, 6, 2, 5, 3, 4):
        loads[i].start()

    def sector_at(offset):
        return lax.rem(me + offset + sectors, sectors)

    def group_at(offset):
        return lax.rem(group + offset, groups)

    def zed_at(offset):
        return lax.rem(zed + offset, ZS)

    def slab_at(offset):
        return lax.rem(slab + offset + slabs, slabs)

    barrier = pltpu.get_barrier_semaphore()
    greeted = 0
    for offset in range(1, HALF + 1):
        for sign in (1, -1):
            pl.semaphore_signal(barrier, inc=1, device_id={"sector": sector_at(sign * offset)})
            greeted += 1
    for offset in range(1, ZS):
        pl.semaphore_signal(barrier, inc=1, device_id={"sector": group * ZS + zed_at(offset)})
        greeted += 1
    for offset in range(1, groups):
        pl.semaphore_signal(barrier, inc=1, device_id={"sector": group_at(offset) * ZS + zed})
        greeted += 1
    for sign in (1, -1):
        pl.semaphore_signal(barrier, inc=1, device_id={"slab": slab_at(sign)})
        greeted += 1

    lanes = lax.broadcasted_iota(jnp.int32, (4, 128), 1)
    quarter = lanes // 32
    odd_lane = lax.rem(lax.broadcasted_iota(jnp.int32, (ZS, 4, 128), 2), 2) == 1
    row_ids = lax.broadcasted_iota(jnp.int32, (16, 128), 0)
    last_slab = slab == slabs - 1
    first_slab = slab == 0

    def share_copy(it, j):
        return pltpu.make_async_remote_copy(
            src_ref=shares.at[it, HALF], dst_ref=shares.at[it, j],
            send_sem=share_send.at[it, j], recv_sem=share_recv.at[it, j],
            device_id={"sector": sector_at(HALF - j)},
        )

    def part_copy(it, j):
        return pltpu.make_async_remote_copy(
            src_ref=partials_out.at[it, j], dst_ref=partials_in.at[it, j],
            send_sem=part_send.at[it, j], recv_sem=part_recv.at[it, j],
            device_id={"sector": sector_at(j - HALF)},
        )

    def edge_copy(it, way):
        return pltpu.make_async_remote_copy(
            src_ref=edge_out.at[it, way], dst_ref=edge_in.at[it, way],
            send_sem=edge_send.at[it, way], recv_sem=edge_recv.at[it, way],
            device_id={"slab": slab_at(1 if way else -1)},
        )

    def zed_copy(it, way, source, offset):
        return pltpu.make_async_remote_copy(
            src_ref=source.at[it, :, zed_at(offset)], dst_ref=mid.at[it, way, :, zed],
            send_sem=band_send.at[it, way, 0, offset], recv_sem=band_recv.at[it, way, 0, offset],
            device_id={"sector": group * ZS + zed_at(offset)},
        )

    def zed_wait(it, way, source, offset):
        pltpu.make_async_remote_copy(
            src_ref=source.at[it, :, zed_at(offset)], dst_ref=mid.at[it, way, :, zed_at(ZS - offset)],
            send_sem=band_send.at[it, way, 0, offset], recv_sem=band_recv.at[it, way, 0, offset],
            device_id={"sector": group * ZS + zed_at(offset)},
        ).wait_recv()

    def group_copy(it, way, dest, offset):
        return pltpu.make_async_remote_copy(
            src_ref=mid.at[it, way, group_at(offset)], dst_ref=dest.at[it, group],
            send_sem=band_send.at[it, way, 1, offset], recv_sem=band_recv.at[it, way, 1, offset],
            device_id={"sector": group_at(offset) * ZS + zed},
        )

    def group_wait(it, way, dest, offset):
        pltpu.make_async_remote_copy(
            src_ref=mid.at[it, way, group_at(offset)], dst_ref=dest.at[it, group_at(groups - offset)],
            send_sem=band_send.at[it, way, 1, offset], recv_sem=band_recv.at[it, way, 1, offset],
            device_id={"sector": group_at(offset) * ZS + zed},
        ).wait_recv()

    def first_hop(it, way, source):
        for offset in range(1, ZS):
            zed_copy(it, way, source, offset).start()
        mid[it, way, :, pl.ds(zed, 1)] = source[it, :, pl.ds(zed, 1)]

    def second_hop(it, way, source, dest):
        for offset in range(1, ZS):
            zed_wait(it, way, source, offset)
        for offset in range(1, groups):
            group_copy(it, way, dest, offset).start()
        dest[it, pl.ds(group, 1)] = mid[it, way, pl.ds(group, 1)]

    def finish_hops(it, way, dest):
        for offset in range(1, groups):
            group_wait(it, way, dest, offset)

    def forward_stop(it, j, step):
        for b in range(blocks):
            out = lax.dot_general(
                shares[it, j, b], tof[j, b], (((1,), (1,)), ((), ())),
                preferred_element_type=jnp.float32,
            )
            n = step * (2 * blocks) + 2 * b
            sums[n] = out[:, :128] + sums[prev_ref[n]]
            sums[n + 1] = out[:, 128:] + sums[prev_ref[n + 1]]

    def adjoint_block(j, b):
        n = j * (2 * blocks) + 2 * b
        picked = jnp.concatenate([dual_half[rows_ref[n]], dual_half[rows_ref[n + 1]]], 1)
        return jnp.dot(picked, tof[j, b], preferred_element_type=jnp.float32)

    sums[terms] = jnp.zeros((16, 128), jnp.float32)

    for t in range(time_blocks):
        span = slice(t * 128, (t + 1) * 128)
        dual = (dual_step * (0.0 - measured_ref[:, span])) / (1.0 + dual_step)
        data_ref[:, span] = dual
        dual_half[t] = dual.astype(jnp.bfloat16)

    pl.semaphore_wait(barrier, greeted)

    def adjoint_sends(it, first):
        def send_stop(i, carry):
            j = far_first(i)
            if first:
                pltpu.make_async_copy(tof_hbm.at[j], tof.at[j], load_sem.at[j]).wait()
            for b in range(blocks):
                partials_out[it, j, b] = adjoint_block(j, b).astype(jnp.bfloat16)
            part_copy(it, j).start()
            return carry

        lax.fori_loop(0, STOPS - 1, send_stop, 0)
        if first:
            loads[HALF].wait()
        for b in range(blocks):
            total[b] = adjoint_block(HALF, b)

    def adjoint_gather(it):
        def add_stop(i, carry):
            j = near_first(i)
            part_copy(it, j).wait_recv()
            for b in range(blocks):
                total[b] = total[b] + partials_in[it, j, b].astype(jnp.float32)
            return carry

        lax.fori_loop(0, STOPS - 1, add_stop, 0)

    def publish(it):
        for b in range(blocks):
            shares[it, HALF, b] = xbar[b].astype(jnp.bfloat16)

        def send(i, carry):
            share_copy(it, far_first(i)).start()
            return carry

        lax.fori_loop(0, STOPS - 1, send, 0)
        for b in range(blocks):
            edge_out[it, 0, pl.ds(b, 1)] = xbar[b, 0:1]
            edge_out[it, 1, pl.ds(b, 1)] = xbar[b, 15:16]
        edge_copy(it, 0).start()
        edge_copy(it, 1).start()
        for b in range(blocks):
            value = xbar[b]
            rolled[b] = value
            for a in range(1, 4):
                rolled[a * blocks + b] = pltpu.roll(value, 32 * a, 1)

        def gather_band(k, carry):
            j = inverse_ref[k]
            block, lane = j // 4, lax.rem(j, 4)
            parts = [
                rolled[lax.rem(r - lane + 4, 4) * blocks + block, 4 * r : 4 * r + 4]
                for r in range(4)
            ]
            low = jnp.where(quarter == 0, parts[0], parts[1])
            high = jnp.where(quarter == 2, parts[2], parts[3])
            bands[it, k // ZS, lax.rem(k, ZS)] = jnp.where(quarter < 2, low, high)
            return carry

        lax.fori_loop(0, sectors, gather_band, 0, unroll=8)
        first_hop(it, 0, bands)

    def haar(upper, lower):
        def pairs(value):
            right = pltpu.roll(value, 127, 2)
            left = pltpu.roll(value, 1, 2)
            return jnp.where(odd_lane, left - value, value + right)

        top, low = pairs(upper), pairs(lower)
        return (top + low) * 0.5, (top - low) * 0.5

    def update_wave(it):
        for g in range(groups):
            full = tiles[it, g]
            upper = jnp.concatenate([full[2 * (i // 2)][None] for i in range(ZS)], 0)
            lower = jnp.concatenate([full[2 * (i // 2) + 1][None] for i in range(ZS)], 0)
            odd = lax.rem(lax.broadcasted_iota(jnp.int32, (ZS, 4, 128), 0), 2) == 1
            top, low = haar(upper, lower)
            coeffs = jnp.where(odd, low, top)
            kept = wave[g] + dual_step * coeffs
            dual = jnp.clip(kept, -wave_limit, wave_limit)
            wave[g] = dual
            upper = jnp.concatenate([dual[2 * (i // 2)][None] for i in range(ZS)], 0)
            lower = jnp.concatenate([dual[2 * (i // 2) + 1][None] for i in range(ZS)], 0)
            top, low = haar(upper, lower)
            back_bands[it, g] = jnp.where(odd, low, top)

    def update_depth(it):
        edge_copy(it, 0).wait_recv()
        edge_copy(it, 1).wait_recv()
        following = edge_in[it, 0]
        previous = edge_in[it, 1]
        for b in range(blocks):
            value = xbar[b]
            up = jnp.where(row_ids == 15, following[b : b + 1], pltpu.roll(value, 15, 0))
            diff = up - value
            diff = jnp.where(jnp.logical_and(last_slab, row_ids == 15), 0.0, diff)
            depth[b] = jnp.clip(depth[b] + dual_step * diff, -depth_limit, depth_limit)
        edge = halo[...] + dual_step * (edge_out[it, 0] - previous)
        edge = jnp.clip(edge, -depth_limit, depth_limit)
        halo[...] = jnp.where(first_slab, 0.0, edge)

    def spread_bands(source, count):
        for g in range(count // ZS):
            value = source(g)
            rolled_back[0, pl.ds(g * ZS, ZS)] = value
            for a in range(1, 4):
                rolled_back[a, pl.ds(g * ZS, ZS)] = pltpu.roll(value, 32 * a, 2)

    def joined_bands(index, b):
        places = [index(4 * b + q) for q in range(4)]
        out = []
        for r in range(4):
            parts = [rolled_back[(q - r) % 4, places[q]] for q in range(4)]
            low = jnp.where(quarter == 0, parts[0], parts[1])
            high = jnp.where(quarter == 2, parts[2], parts[3])
            out.append(jnp.where(quarter < 2, low, high))
        return out

    adjoint_sends(0, True)
    adjoint_gather(0)
    for b in range(blocks):
        image = jnp.maximum(0.0 - primal_step * total[b], 0.0)
        image_ref[:, b * 128 : (b + 1) * 128] = image
        xbar[b] = 2.0 * image
        depth[b] = jnp.zeros((16, 128), jnp.float32)
    halo[...] = jnp.zeros_like(halo)
    wave[...] = jnp.zeros_like(wave)

    def iteration(it, carry):
        publish(it)
        forward_stop(it, HALF, 0)

        def early(i, carry):
            j = near_first(i)
            share_copy(it, j).wait_recv()
            forward_stop(it, j, i + 1)
            return carry

        lax.fori_loop(0, 3, early, 0)
        second_hop(it, 0, bands, tiles)
        lax.fori_loop(3, STOPS - 1, early, 0)
        for t in range(time_blocks):
            span = slice(t * 128, (t + 1) * 128)
            moved = sums[prev_ref[terms + t]] - measured_ref[:, span]
            dual = (data_ref[:, span] + dual_step * moved) / (1.0 + dual_step)
            data_ref[:, span] = dual
            dual_half[t] = dual.astype(jnp.bfloat16)
        adjoint_sends(it + 1, False)
        finish_hops(it, 0, tiles)
        update_wave(it)
        first_hop(it, 1, back_bands)
        update_depth(it)
        second_hop(it, 1, back_bands, wave_back)
        adjoint_gather(it + 1)
        finish_hops(it, 1, wave_back)
        spread_bands(lambda g: wave_back[it, g], sectors)
        for b in range(blocks):
            for r, part in enumerate(joined_bands(lambda j: owner_ref[j], b)):
                total[b, 4 * r : 4 * r + 4] = total[b, 4 * r : 4 * r + 4] + part
        for b in range(blocks):
            span = slice(b * 128, (b + 1) * 128)
            shifted = jnp.where(row_ids == 0, halo[b : b + 1], pltpu.roll(depth[b], 1, 0))
            update = total[b] + (shifted - depth[b])
            old = image_ref[:, span]
            image = jnp.maximum(old - primal_step * update, 0.0)
            xbar[b] = 2.0 * image - old
            image_ref[:, span] = image
        return carry

    lax.fori_loop(0, ITERS - 1, iteration, 0)

    spread_bands(lambda g: wave[g], sectors)
    for b in range(blocks):
        for r, part in enumerate(joined_bands(lambda j: j, b)):
            wave_ref[4 * r : 4 * r + 4, b * 128 : (b + 1) * 128] = part

    def drain(i, carry):
        j = far_first(i)
        for it in range(ITERS):
            part_copy(it, j).wait_send()
        for it in range(ITERS - 1):
            share_copy(it, j).wait_send()
        return carry

    lax.fori_loop(0, STOPS - 1, drain, 0)
    for it in range(ITERS - 1):
        edge_copy(it, 0).wait_send()
        edge_copy(it, 1).wait_send()
        for way, source, dest in ((0, bands, tiles), (1, back_bands, wave_back)):
            for offset in range(1, ZS):
                zed_copy(it, way, source, offset).wait_send()
            for offset in range(1, groups):
                group_copy(it, way, dest, offset).wait_send()


def body(measured, tof, tof_rows, tile_owner):
    stops, blocks, slots, width, _ = tof.shape
    depth_rows = measured.shape[0]
    time_blocks = measured.shape[1] // width
    pixels = blocks * width
    sectors = lax.axis_size("sector")
    slabs = lax.axis_size("slab")
    groups = sectors // ZS
    terms = stops * blocks * slots
    met = [HALF] + [far_first(i) for i in range(STOPS - 2, -1, -1)]
    rows = jnp.concatenate([tof_rows[j].reshape(-1) for j in met])
    order = jnp.arange(terms, dtype=jnp.int32)
    wanted = jnp.concatenate([rows, jnp.arange(time_blocks, dtype=jnp.int32)])
    limit = jnp.concatenate([order, jnp.full((time_blocks,), terms, jnp.int32)])
    match = jnp.logical_and(rows[None] == wanted[:, None], order[None] < limit[:, None])
    prev = jnp.max(jnp.where(match, order[None], -1), 1)
    prev = jnp.where(prev < 0, terms, prev)
    bands = jnp.arange(sectors, dtype=jnp.int32)
    inverse = jnp.sum(jnp.where(tile_owner[None] == bands[:, None], bands[None], 0), 1)

    vmem = pl.BlockSpec(memory_space=pltpu.VMEM)
    smem = pl.BlockSpec(memory_space=pltpu.SMEM)
    f32, half = jnp.float32, jnp.bfloat16
    field = (blocks, depth_rows, width)
    again = ITERS - 1
    ring = (groups, ZS, depth_rows // 4, width)
    return pl.pallas_call(
        functools.partial(kernel, sectors, groups, slabs, blocks, time_blocks),
        out_shape=(
            jax.ShapeDtypeStruct((depth_rows, pixels), f32),
            jax.ShapeDtypeStruct(measured.shape, f32),
            jax.ShapeDtypeStruct((depth_rows, pixels), f32),
        ),
        in_specs=[smem] * 4 + [vmem, pl.BlockSpec(memory_space=pl.ANY)],
        out_specs=(vmem, vmem, vmem),
        scratch_shapes=[
            pltpu.VMEM((stops, blocks, slots * width, width), half),
            pltpu.VMEM((terms + 1, depth_rows, width), f32),
            pltpu.VMEM((time_blocks, depth_rows, width), half),
            pltpu.VMEM(field, f32),
            pltpu.VMEM(field, f32),
            pltpu.VMEM((blocks, width), f32),
            pltpu.VMEM(field, f32),
            pltpu.VMEM((again, stops) + field, half),
            pltpu.VMEM((ITERS, stops) + field, half),
            pltpu.VMEM((ITERS, stops) + field, half),
            pltpu.VMEM((again, 2, blocks, width), f32),
            pltpu.VMEM((again, 2, blocks, width), f32),
            pltpu.VMEM((4 * blocks, depth_rows, width), f32),
            pltpu.VMEM((again,) + ring, f32),
            pltpu.VMEM((again, 2) + ring, f32),
            pltpu.VMEM((again,) + ring, f32),
            pltpu.VMEM(ring, f32),
            pltpu.VMEM((4, sectors, depth_rows // 4, width), f32),
            pltpu.VMEM((again,) + ring, f32),
            pltpu.VMEM((again,) + ring, f32),
            pltpu.SemaphoreType.DMA((stops,)),
            pltpu.SemaphoreType.DMA((again, stops)),
            pltpu.SemaphoreType.DMA((again, stops)),
            pltpu.SemaphoreType.DMA((ITERS, stops)),
            pltpu.SemaphoreType.DMA((ITERS, stops)),
            pltpu.SemaphoreType.DMA((again, 2)),
            pltpu.SemaphoreType.DMA((again, 2)),
            pltpu.SemaphoreType.DMA((again, 2, 2, ZS)),
            pltpu.SemaphoreType.DMA((again, 2, 2, ZS)),
        ],
        compiler_params=pltpu.CompilerParams(
            collective_id=0, has_side_effects=True, vmem_limit_bytes=48 * 1024 * 1024
        ),
    )(tof_rows.reshape(-1), prev, tile_owner, inverse, measured, tof.reshape(stops, blocks, slots * width, width))


def solution(mesh):
    return jax.shard_map(
        body,
        mesh=mesh,
        in_specs=(
            P("slab", "sector"),
            P("sector", None, None, None, None),
            P("sector", None, None),
            P(),
        ),
        out_specs=(P("slab", "sector"), P("slab", "sector"), P("slab", "sector")),
        check_vma=False,
    )
```

time: 666 us -> 122 us (0.18); the launches traced: 654 us -> 120 us
  waiting for transfers between devices: 272 us -> 0 us
  starting transfers between devices: 219 us -> 0 us
  Pallas kernels: 0 us -> 111 us
  matrix products: 75.3 us -> 0 us
  local copies, waits for them, and re-layouts: 66.8 us -> 6.92 us
  other arithmetic: 18.5 us -> 1.69 us
    ppermute x54 -> x0, waiting for transfers between devices: 272 us -> none  [the longest x48 272 us: shifted(): lax.ppermute(shard, axis, [(i, (i + by) % length) for i in range(length)])]
    ppermute x54 -> x0, starting transfers between devices: 183 us -> none  [the longest x48 171 us: shifted(): lax.ppermute(shard, axis, [(i, (i + by) % length) for i in range(length)])]
    pallas_call x0 -> x1, Pallas kernels: none -> 111 us  [body(): pl.pallas_call(functools.partial(kernel, sectors, groups, slabs, blocks,...]
    dot_general x54 -> x0, matrix products: 75.3 us -> none  [the longest x24 38.4 us: contribute(): jnp.einsum('dbp,bkrp->dbkr', shaped, tof[stop_at], preferred_element_type...]
    all_to_all x6 -> x0, starting transfers between devices: 36.1 us -> none  [the longest x3 22 us: body(): lax.all_to_all(outgoing, 'sector', split_axis=1, concat_axis=1, tiled=True)]
    unnamed x132 -> x8, local copies, waits for them, and re-layouts: 27.7 us -> 4.43 us
    gather x33 -> x0, local copies, waits for them, and re-layouts: 19.5 us -> none  [the longest x24 14.6 us: pull(): dual_half.reshape(depth_rows, time_blocks, width)[:, tof_rows[stop_at]]]
  transfers between devices with their start and end apart: 60 -> 0, of which waited for: 44 -> 0; matrix products, arithmetic and copies ran while one was open for 23% -> 0% of each run, Pallas kernels for 0% -> 0%
where the time goes in v1:
time: 122 us; the launch traced here: 120 us
  Pallas kernels  111 us (91%)
  local copies, waits for them, and re-layouts  6.92 us (6%)
  other arithmetic  1.69 us (1%)
    pallas_call x1, Pallas kernels, body(): pl.pallas_call(functools.partial(kernel, sectors, groups, slabs, blocks,...  111 us
    unnamed x8, local copies, waits for them, and re-layouts  4.43 us

profile of v1, /device:TPU:8, one launch (start us, length us, event | category | flops | bytes accessed | tf_op | source)
XLA Modules:
  0.0 120.5 jit_solution(22549982097452478)
XLA Ops:
  0.6 0.8 select_reduce_fusion.1.inverse_ref
  1.4 0.8 fusion.1
  2.2 0.1 copy.32
  2.3 0.1 reshape_squeeze.31
  2.4 0.1 copy.30
  2.5 0.1 reshape_squeeze.29
  2.6 0.1 copy.29
  2.6 0.1 reshape_squeeze.28
  2.7 0.1 copy.28
  2.8 0.1 reshape_squeeze.27
  2.9 0.1 copy.27
  3.0 0.1 reshape_squeeze.26
  3.1 0.1 copy.26
  3.2 0.1 reshape_squeeze.25
  3.3 0.1 copy.25
  3.3 0.1 reshape_squeeze.24
  3.4 0.1 copy.31
  3.5 0.1 reshape_squeeze.30
  3.6 0.1 concatenate.8
  3.7 0.1 concatenate.9
  3.8 0.9 select_reduce_fusion
  4.7 0.8 copy.24
  5.5 0.1 reshape.16.rows_ref
  5.7 0.0 copy-start
  5.7 0.9 copy-done
  6.6 0.0 copy-start.1
  6.6 0.7 copy-done.1
  7.3 111.2 %shard_map.67 = (f32[16,2048]{1,0:T(8,128)S(1)}, f32[16,4096]{1,0:T(8,128)S(1)}, f32[16,2048]{1,0:T(8,128)S(1)}) custom-call(s32[256]{0:T(256)S(1)} %reshape.16.rows_ref, s32[288]{0:T(512)S(1)} %compare_select_fusion.prev_ref, s32[64]{0:T(128)S(1)} %copy-done.1, s32[64]{0:T(128)S(1)} %select_reduce_fusion.1.inverse_ref, f32[16,4096]{1,0:T(8,128)S(1)} %copy-done, ...), custom_call_target="tpu_custom_call" | custom-call | tf_op jit(solution)/shard_map/pallas_call | solution.py:396
  118.5 0.7 copy.36
  119.1 0.7 copy.37
  119.8 0.7 copy.38
  (2 shorter events, 0.0 us)
Async XLA Ops:
  5.7 1.0 copy-start
  6.6 0.7 copy-start.1

commit v2 on v1

--- a/solution.py
+++ b/solution.py
@@ -2,6 +2,7 @@
 
 import jax
 import jax.numpy as jnp
+import numpy as np
 from jax import lax
 from jax.experimental import pallas as pl
 from jax.experimental.pallas import tpu as pltpu
@@ -18,12 +19,18 @@
 depth_limit = 0.5
 
 
-def far_first(i):
-    return (i % 2) * (STOPS - 1) + (1 - 2 * (i % 2)) * (i // 2)
-
-
-def near_first(i):
-    return far_first(6 - i)
+CHUNKS = 4
+
+
+def term_place(stop, block, slot, blocks):
+    size = blocks // CHUNKS
+    chunk, inside = block // size, 2 * (block % size) + slot
+    step = abs(stop - HALF)
+    if step == 0:
+        return 2 * block + slot
+    both = step < HALF
+    base = 2 * blocks * (2 * step - 1) + chunk * 2 * size * (2 if both else 1)
+    return base + (2 * size if stop > HALF else 0) + inside
 
 
 def kernel(
@@ -31,15 +38,16 @@
     rows_ref, prev_ref, owner_ref, inverse_ref, measured_ref, tof_hbm,
     image_ref, data_ref, wave_ref,
     tof, sums, dual_half, xbar, depth, halo, total,
-    shares, partials_out, partials_in, edge_out, edge_in,
+    shares, part_out, part_in, last_out, last_in, edge_out, edge_in,
     rolled, bands, mid, tiles, wave, rolled_back, back_bands, wave_back,
-    load_sem, share_send, share_recv, part_send, part_recv, edge_send, edge_recv,
+    load_sem, share_send, share_recv, part_send, part_recv, last_send, last_recv, edge_send, edge_recv,
     band_send, band_recv,
 ):
     me = lax.axis_index("sector")
     slab = lax.axis_index("slab")
     group, zed = me // ZS, lax.rem(me, ZS)
     terms = STOPS * blocks * 2
+    size = blocks // CHUNKS
 
     loads = [
         pltpu.make_async_copy(tof_hbm.at[j], tof.at[j], load_sem.at[j]) for j in range(STOPS)
@@ -61,10 +69,9 @@
 
     barrier = pltpu.get_barrier_semaphore()
     greeted = 0
-    for offset in range(1, HALF + 1):
-        for sign in (1, -1):
-            pl.semaphore_signal(barrier, inc=1, device_id={"sector": sector_at(sign * offset)})
-            greeted += 1
+    for sign in (1, -1):
+        pl.semaphore_signal(barrier, inc=1, device_id={"sector": sector_at(sign)})
+        greeted += 1
     for offset in range(1, ZS):
         pl.semaphore_signal(barrier, inc=1, device_id={"sector": group * ZS + zed_at(offset)})
         greeted += 1
@@ -82,18 +89,30 @@
     last_slab = slab == slabs - 1
     first_slab = slab == 0
 
-    def share_copy(it, j):
+    def share_copy(it, j, c):
+        way = 1 if j < HALF else -1
+        part = pl.ds(c * size, size)
         return pltpu.make_async_remote_copy(
-            src_ref=shares.at[it, HALF], dst_ref=shares.at[it, j],
-            send_sem=share_send.at[it, j], recv_sem=share_recv.at[it, j],
-            device_id={"sector": sector_at(HALF - j)},
-        )
-
-    def part_copy(it, j):
+            src_ref=shares.at[it, j + way, part], dst_ref=shares.at[it, j, part],
+            send_sem=share_send.at[it, j, c], recv_sem=share_recv.at[it, j, c],
+            device_id={"sector": sector_at(way)},
+        )
+
+    def part_copy(it, j, c):
+        way = 1 if j > HALF else -1
+        part = pl.ds(c * size, size)
         return pltpu.make_async_remote_copy(
-            src_ref=partials_out.at[it, j], dst_ref=partials_in.at[it, j],
-            send_sem=part_send.at[it, j], recv_sem=part_recv.at[it, j],
-            device_id={"sector": sector_at(j - HALF)},
+            src_ref=part_out.at[it, j, part], dst_ref=part_in.at[it, j, part],
+            send_sem=part_send.at[it, j, c], recv_sem=part_recv.at[it, j, c],
+            device_id={"sector": sector_at(way)},
+        )
+
+    def last_copy(it, side, c):
+        part = pl.ds(c * size, size)
+        return pltpu.make_async_remote_copy(
+            src_ref=last_out.at[it, side, part], dst_ref=last_in.at[it, side, part],
+            send_sem=last_send.at[it, side, c], recv_sem=last_recv.at[it, side, c],
+            device_id={"sector": sector_at(1 if side else -1)},
         )
 
     def edge_copy(it, way):
@@ -147,15 +166,14 @@
         for offset in range(1, groups):
             group_wait(it, way, dest, offset)
 
-    def forward_stop(it, j, step):
-        for b in range(blocks):
-            out = lax.dot_general(
-                shares[it, j, b], tof[j, b], (((1,), (1,)), ((), ())),
-                preferred_element_type=jnp.float32,
-            )
-            n = step * (2 * blocks) + 2 * b
-            sums[n] = out[:, :128] + sums[prev_ref[n]]
-            sums[n + 1] = out[:, 128:] + sums[prev_ref[n + 1]]
+    def forward_block(it, j, b, place):
+        out = lax.dot_general(
+            shares[it, j, b], tof[j, b], (((1,), (1,)), ((), ())),
+            preferred_element_type=jnp.float32,
+        )
+        n = j * (2 * blocks) + 2 * b
+        sums[place] = out[:, :128] + sums[prev_ref[n]]
+        sums[place + 1] = out[:, 128:] + sums[prev_ref[n + 1]]
 
     def adjoint_block(j, b):
         n = j * (2 * blocks) + 2 * b
@@ -172,41 +190,85 @@
 
     pl.semaphore_wait(barrier, greeted)
 
-    def adjoint_sends(it, first):
-        def send_stop(i, carry):
-            j = far_first(i)
-            if first:
-                pltpu.make_async_copy(tof_hbm.at[j], tof.at[j], load_sem.at[j]).wait()
-            for b in range(blocks):
-                partials_out[it, j, b] = adjoint_block(j, b).astype(jnp.bfloat16)
-            part_copy(it, j).start()
+    def adjoint_step(it, step, first):
+        down, up = step, STOPS - 1 - step
+        if first:
+            loads[down].wait()
+            loads[up].wait()
+
+        def chunk(c, carry):
+            lower = [adjoint_block(down, c * size + i) for i in range(size)]
+            upper = [adjoint_block(up, c * size + i) for i in range(size)]
+            if step > 0:
+                part_copy(it, down - 1, c).wait_recv()
+                for i in range(size):
+                    lower[i] = lower[i] + part_in[it, down - 1, c * size + i].astype(jnp.float32)
+            if step < HALF - 1:
+                for i in range(size):
+                    part_out[it, down, c * size + i] = lower[i].astype(jnp.bfloat16)
+                part_copy(it, down, c).start()
+            else:
+                for i in range(size):
+                    last_out[it, 0, c * size + i] = lower[i]
+                last_copy(it, 0, c).start()
+            if step == HALF - 1:
+                for i in range(size):
+                    total[c * size + i] = upper[i]
+                return carry
+            if step > 0:
+                part_copy(it, up + 1, c).wait_recv()
+                for i in range(size):
+                    upper[i] = upper[i] + part_in[it, up + 1, c * size + i].astype(jnp.float32)
+            if step < HALF - 2:
+                for i in range(size):
+                    part_out[it, up, c * size + i] = upper[i].astype(jnp.bfloat16)
+                part_copy(it, up, c).start()
+            else:
+                for i in range(size):
+                    last_out[it, 1, c * size + i] = upper[i]
+                last_copy(it, 1, c).start()
             return carry
 
-        lax.fori_loop(0, STOPS - 1, send_stop, 0)
-        if first:
-            loads[HALF].wait()
-        for b in range(blocks):
-            total[b] = adjoint_block(HALF, b)
-
-    def adjoint_gather(it):
-        def add_stop(i, carry):
-            j = near_first(i)
-            part_copy(it, j).wait_recv()
-            for b in range(blocks):
-                total[b] = total[b] + partials_in[it, j, b].astype(jnp.float32)
+        lax.fori_loop(0, CHUNKS, chunk, 0)
+
+    def back_block(it, b):
+        return total[b] + last_in[it, 1, b] + last_in[it, 0, b]
+
+    def arrived(it, c):
+        last_copy(it, 1, c).wait_recv()
+        last_copy(it, 0, c).wait_recv()
+
+    def forward_own(it):
+        def chunk(c, carry):
+            for i in range(size):
+                b = c * size + i
+                forward_block(it, HALF, b, 2 * b)
             return carry
 
-        lax.fori_loop(0, STOPS - 1, add_stop, 0)
+        lax.fori_loop(0, CHUNKS, chunk, 0)
+
+    def forward_step(it, step):
+        down, up = HALF + step, HALF - step
+        sides = (up, down) if step < HALF else (up,)
+
+        def chunk(c, carry):
+            for j in sides:
+                share_copy(it, j, c).wait_recv()
+                if 0 < j < STOPS - 1:
+                    share_copy(it, j + (1 if j > HALF else -1), c).start()
+                place = term_place(j, 0, 0, blocks) + c * (2 * size * len(sides))
+                for i in range(size):
+                    forward_block(it, j, c * size + i, place + 2 * i)
+            return carry
+
+        lax.fori_loop(0, CHUNKS, chunk, 0)
 
     def publish(it):
-        for b in range(blocks):
-            shares[it, HALF, b] = xbar[b].astype(jnp.bfloat16)
-
-        def send(i, carry):
-            share_copy(it, far_first(i)).start()
-            return carry
-
-        lax.fori_loop(0, STOPS - 1, send, 0)
+        for c in range(CHUNKS):
+            for b in range(c * size, (c + 1) * size):
+                shares[it, HALF, b] = xbar[b].astype(jnp.bfloat16)
+            share_copy(it, HALF - 1, c).start()
+            share_copy(it, HALF + 1, c).start()
         for b in range(blocks):
             edge_out[it, 0, pl.ds(b, 1)] = xbar[b, 0:1]
             edge_out[it, 1, pl.ds(b, 1)] = xbar[b, 15:16]
@@ -290,10 +352,12 @@
             out.append(jnp.where(quarter < 2, low, high))
         return out
 
-    adjoint_sends(0, True)
-    adjoint_gather(0)
+    for step in range(HALF):
+        adjoint_step(0, step, True)
+    for c in range(CHUNKS):
+        arrived(0, c)
     for b in range(blocks):
-        image = jnp.maximum(0.0 - primal_step * total[b], 0.0)
+        image = jnp.maximum(0.0 - primal_step * back_block(0, b), 0.0)
         image_ref[:, b * 128 : (b + 1) * 128] = image
         xbar[b] = 2.0 * image
         depth[b] = jnp.zeros((16, 128), jnp.float32)
@@ -302,39 +366,38 @@
 
     def iteration(it, carry):
         publish(it)
-        forward_stop(it, HALF, 0)
-
-        def early(i, carry):
-            j = near_first(i)
-            share_copy(it, j).wait_recv()
-            forward_stop(it, j, i + 1)
-            return carry
-
-        lax.fori_loop(0, 3, early, 0)
+        forward_own(it)
+        forward_step(it, 1)
+        forward_step(it, 2)
         second_hop(it, 0, bands, tiles)
-        lax.fori_loop(3, STOPS - 1, early, 0)
+        forward_step(it, 3)
+        forward_step(it, 4)
         for t in range(time_blocks):
             span = slice(t * 128, (t + 1) * 128)
             moved = sums[prev_ref[terms + t]] - measured_ref[:, span]
             dual = (data_ref[:, span] + dual_step * moved) / (1.0 + dual_step)
             data_ref[:, span] = dual
             dual_half[t] = dual.astype(jnp.bfloat16)
-        adjoint_sends(it + 1, False)
+        adjoint_step(it + 1, 0, False)
         finish_hops(it, 0, tiles)
         update_wave(it)
         first_hop(it, 1, back_bands)
+        adjoint_step(it + 1, 1, False)
         update_depth(it)
+        adjoint_step(it + 1, 2, False)
         second_hop(it, 1, back_bands, wave_back)
-        adjoint_gather(it + 1)
+        adjoint_step(it + 1, 3, False)
         finish_hops(it, 1, wave_back)
         spread_bands(lambda g: wave_back[it, g], sectors)
         for b in range(blocks):
             for r, part in enumerate(joined_bands(lambda j: owner_ref[j], b)):
                 total[b, 4 * r : 4 * r + 4] = total[b, 4 * r : 4 * r + 4] + part
+        for c in range(CHUNKS):
+            arrived(it + 1, c)
         for b in range(blocks):
             span = slice(b * 128, (b + 1) * 128)
             shifted = jnp.where(row_ids == 0, halo[b : b + 1], pltpu.roll(depth[b], 1, 0))
-            update = total[b] + (shifted - depth[b])
+            update = back_block(it + 1, b) + (shifted - depth[b])
             old = image_ref[:, span]
             image = jnp.maximum(old - primal_step * update, 0.0)
             xbar[b] = 2.0 * image - old
@@ -348,15 +411,21 @@
         for r, part in enumerate(joined_bands(lambda j: j, b)):
             wave_ref[4 * r : 4 * r + 4, b * 128 : (b + 1) * 128] = part
 
-    def drain(i, carry):
-        j = far_first(i)
+    def drain(c, carry):
+        for j in range(STOPS):
+            if j == HALF:
+                continue
+            for it in range(ITERS - 1):
+                share_copy(it, j, c).wait_send()
+            if j not in (HALF - 1, HALF + 1):
+                for it in range(ITERS):
+                    part_copy(it, j, c).wait_send()
         for it in range(ITERS):
-            part_copy(it, j).wait_send()
-        for it in range(ITERS - 1):
-            share_copy(it, j).wait_send()
+            last_copy(it, 0, c).wait_send()
+            last_copy(it, 1, c).wait_send()
         return carry
 
-    lax.fori_loop(0, STOPS - 1, drain, 0)
+    lax.fori_loop(0, CHUNKS, drain, 0)
     for it in range(ITERS - 1):
         edge_copy(it, 0).wait_send()
         edge_copy(it, 1).wait_send()
@@ -376,13 +445,21 @@
     slabs = lax.axis_size("slab")
     groups = sectors // ZS
     terms = stops * blocks * slots
-    met = [HALF] + [far_first(i) for i in range(STOPS - 2, -1, -1)]
-    rows = jnp.concatenate([tof_rows[j].reshape(-1) for j in met])
-    order = jnp.arange(terms, dtype=jnp.int32)
+    rows = tof_rows.reshape(-1)
+    place = np.array(
+        [
+            term_place(j, b, k, blocks)
+            for j in range(stops)
+            for b in range(blocks)
+            for k in range(slots)
+        ],
+        np.int32,
+    )
     wanted = jnp.concatenate([rows, jnp.arange(time_blocks, dtype=jnp.int32)])
-    limit = jnp.concatenate([order, jnp.full((time_blocks,), terms, jnp.int32)])
-    match = jnp.logical_and(rows[None] == wanted[:, None], order[None] < limit[:, None])
-    prev = jnp.max(jnp.where(match, order[None], -1), 1)
+    limit = jnp.asarray(np.concatenate([place, np.full((time_blocks,), terms, np.int32)]))
+    place = jnp.asarray(place)
+    match = jnp.logical_and(rows[None] == wanted[:, None], place[None] < limit[:, None])
+    prev = jnp.max(jnp.where(match, place[None], -1), 1)
     prev = jnp.where(prev < 0, terms, prev)
     bands = jnp.arange(sectors, dtype=jnp.int32)
     inverse = jnp.sum(jnp.where(tile_owner[None] == bands[:, None], bands[None], 0), 1)
@@ -413,6 +490,8 @@
             pltpu.VMEM((again, stops) + field, half),
             pltpu.VMEM((ITERS, stops) + field, half),
             pltpu.VMEM((ITERS, stops) + field, half),
+            pltpu.VMEM((ITERS, 2) + field, f32),
+            pltpu.VMEM((ITERS, 2) + field, f32),
             pltpu.VMEM((again, 2, blocks, width), f32),
             pltpu.VMEM((again, 2, blocks, width), f32),
             pltpu.VMEM((4 * blocks, depth_rows, width), f32),
@@ -424,10 +503,12 @@
             pltpu.VMEM((again,) + ring, f32),
             pltpu.VMEM((again,) + ring, f32),
             pltpu.SemaphoreType.DMA((stops,)),
-            pltpu.SemaphoreType.DMA((again, stops)),
-            pltpu.SemaphoreType.DMA((again, stops)),
-            pltpu.SemaphoreType.DMA((ITERS, stops)),
-            pltpu.SemaphoreType.DMA((ITERS, stops)),
+            pltpu.SemaphoreType.DMA((again, stops, CHUNKS)),
+            pltpu.SemaphoreType.DMA((again, stops, CHUNKS)),
+            pltpu.SemaphoreType.DMA((ITERS, stops, CHUNKS)),
+            pltpu.SemaphoreType.DMA((ITERS, stops, CHUNKS)),
+            pltpu.SemaphoreType.DMA((ITERS, 2, CHUNKS)),
+            pltpu.SemaphoreType.DMA((ITERS, 2, CHUNKS)),
             pltpu.SemaphoreType.DMA((again, 2)),
             pltpu.SemaphoreType.DMA((again, 2)),
             pltpu.SemaphoreType.DMA((again, 2, 2, ZS)),
@@ -436,7 +517,7 @@
         compiler_params=pltpu.CompilerParams(
             collective_id=0, has_side_effects=True, vmem_limit_bytes=48 * 1024 * 1024
         ),
-    )(tof_rows.reshape(-1), prev, tile_owner, inverse, measured, tof.reshape(stops, blocks, slots * width, width))
+    )(rows, prev, tile_owner, inverse, measured, tof.reshape(stops, blocks, slots * width, width))
 
 
 def solution(mesh):

time: 122 us -> 128 us (1.049)
  Pallas kernels: 111 us -> 119 us
  local copies, waits for them, and re-layouts: 6.92 us -> 4.57 us
    pallas_call x1, Pallas kernels: 111 us -> 119 us  [body(): pl.pallas_call(functools.partial(kernel, sectors, groups, slabs, blocks,...]
    slice x9 -> x0, local copies, waits for them, and re-layouts: 1.47 us -> none  [body(): rows = jnp.concatenate([tof_rows[j].reshape(-1) for j in met])]
where the time goes in v2:
time: 128 us; the launch traced here: 126 us
  Pallas kernels  119 us (93%)
  local copies, waits for them, and re-layouts  4.57 us (4%)
  other arithmetic  1.71 us (1%)
    pallas_call x1, Pallas kernels, body(): pl.pallas_call(functools.partial(kernel, sectors, groups, slabs, blocks,...  119 us
    unnamed x8, local copies, waits for them, and re-layouts  4.43 us

profile of v2, /device:TPU:8, one launch (start us, length us, event | category | flops | bytes accessed | tf_op | source)
XLA Modules:
  0.0 126.4 jit_solution(12868073217197815791)
XLA Ops:
  0.6 0.8 select_reduce_fusion.1.inverse_ref
  1.4 0.8 copy.10
  2.2 0.1 reshape.17.rows_ref
  2.4 0.9 select_reduce_fusion
  3.3 0.0 copy-start
  3.3 0.9 copy-done
  4.3 0.0 copy-start.1
  4.3 0.7 copy-done.1
  4.9 119.5 %shard_map.85 = (f32[16,2048]{1,0:T(8,128)S(1)}, f32[16,4096]{1,0:T(8,128)S(1)}, f32[16,2048]{1,0:T(8,128)S(1)}) custom-call(s32[256]{0:T(256)S(1)} %reshape.17.rows_ref, s32[288]{0:T(512)S(1)} %compare_select_fusion.prev_ref, s32[64]{0:T(128)S(1)} %copy-done.1, s32[64]{0:T(128)S(1)} %select_reduce_fusion.1.inverse_ref, f32[16,4096]{1,0:T(8,128)S(1)} %copy-done, ...), custom_call_target="tpu_custom_call" | custom-call | tf_op jit(solution)/shard_map/pallas_call | solution.py:473
  124.4 0.7 copy.14
  125.1 0.7 copy.15
  125.8 0.7 copy.16
  (3 shorter events, 0.0 us)
Async XLA Ops:
  3.3 1.0 copy-start
  4.3 0.7 copy-start.1

commit v3 on v1

--- a/solution.py
+++ b/solution.py
@@ -18,22 +18,20 @@
 depth_limit = 0.5
 
 
-def far_first(i):
-    return (i % 2) * (STOPS - 1) + (1 - 2 * (i % 2)) * (i // 2)
-
-
-def near_first(i):
-    return far_first(6 - i)
+MET = (4, 2, 6, 3, 5, 1, 7, 0)
+SENT = (0, 1, 7, 3, 5, 2, 6, 4)
+HOPS = {0: -2, 1: -1, 7: 1, 3: -1, 5: 1, 2: -2, 6: 2}
+UNROLL = 8
 
 
 def kernel(
     sectors, groups, slabs, blocks, time_blocks,
-    rows_ref, prev_ref, owner_ref, inverse_ref, measured_ref, tof_hbm,
+    rows_ref, owner_ref, rows_block, owner_block, measured_hbm, tof_hbm,
     image_ref, data_ref, wave_ref,
-    tof, sums, dual_half, xbar, depth, halo, total,
-    shares, partials_out, partials_in, edge_out, edge_in,
+    tof, measured_ref, prev_block, last_block, inverse_block, prev_ref, last_ref, inverse_ref, sums, dual_half, xbar, depth, halo, total,
+    shares, part_out, part_in, relay, edge_out, edge_in,
     rolled, bands, mid, tiles, wave, rolled_back, back_bands, wave_back,
-    load_sem, share_send, share_recv, part_send, part_recv, edge_send, edge_recv,
+    load_sem, index_sem, share_send, share_recv, part_send, part_recv, edge_send, edge_recv,
     band_send, band_recv,
 ):
     me = lax.axis_index("sector")
@@ -44,8 +42,10 @@
     loads = [
         pltpu.make_async_copy(tof_hbm.at[j], tof.at[j], load_sem.at[j]) for j in range(STOPS)
     ]
-    for i in (0, 7, 1, 6, 2, 5, 3, 4):
-        loads[i].start()
+    measured_load = pltpu.make_async_copy(measured_hbm, measured_ref, load_sem.at[STOPS])
+    measured_load.start()
+    for j in SENT:
+        loads[j].start()
 
     def sector_at(offset):
         return lax.rem(me + offset + sectors, sectors)
@@ -61,10 +61,9 @@
 
     barrier = pltpu.get_barrier_semaphore()
     greeted = 0
-    for offset in range(1, HALF + 1):
-        for sign in (1, -1):
-            pl.semaphore_signal(barrier, inc=1, device_id={"sector": sector_at(sign * offset)})
-            greeted += 1
+    for hop in (1, -1, 2, -2):
+        pl.semaphore_signal(barrier, inc=1, device_id={"sector": sector_at(hop)})
+        greeted += 1
     for offset in range(1, ZS):
         pl.semaphore_signal(barrier, inc=1, device_id={"sector": group * ZS + zed_at(offset)})
         greeted += 1
@@ -83,17 +82,18 @@
     first_slab = slab == 0
 
     def share_copy(it, j):
+        source = {3: HALF, 5: HALF, 2: HALF, 6: HALF, 1: 2, 0: 2, 7: 6}[j]
         return pltpu.make_async_remote_copy(
-            src_ref=shares.at[it, HALF], dst_ref=shares.at[it, j],
+            src_ref=shares.at[it, source], dst_ref=shares.at[it, j],
             send_sem=share_send.at[it, j], recv_sem=share_recv.at[it, j],
-            device_id={"sector": sector_at(HALF - j)},
+            device_id={"sector": sector_at(source - j)},
         )
 
     def part_copy(it, j):
         return pltpu.make_async_remote_copy(
-            src_ref=partials_out.at[it, j], dst_ref=partials_in.at[it, j],
+            src_ref=part_out.at[it, j], dst_ref=part_in.at[it, j],
             send_sem=part_send.at[it, j], recv_sem=part_recv.at[it, j],
-            device_id={"sector": sector_at(j - HALF)},
+            device_id={"sector": sector_at(HOPS[j])},
         )
 
     def edge_copy(it, way):
@@ -147,22 +147,20 @@
         for offset in range(1, groups):
             group_wait(it, way, dest, offset)
 
-    def forward_stop(it, j, step):
-        for b in range(blocks):
-            out = lax.dot_general(
-                shares[it, j, b], tof[j, b], (((1,), (1,)), ((), ())),
-                preferred_element_type=jnp.float32,
-            )
-            n = step * (2 * blocks) + 2 * b
-            sums[n] = out[:, :128] + sums[prev_ref[n]]
-            sums[n + 1] = out[:, 128:] + sums[prev_ref[n + 1]]
+    def forward_block(it, j, b, place):
+        out = lax.dot_general(
+            shares[it, j, b], tof[j, b], (((1,), (1,)), ((), ())),
+            preferred_element_type=jnp.float32,
+        )
+        sums[place] = out[:, :128] + sums[prev_ref[0, place]]
+        sums[place + blocks] = out[:, 128:]
 
     def adjoint_block(j, b):
-        n = j * (2 * blocks) + 2 * b
-        picked = jnp.concatenate([dual_half[rows_ref[n]], dual_half[rows_ref[n + 1]]], 1)
+        picked = jnp.concatenate([dual_half[rows_ref[j, 0, b]], dual_half[rows_ref[j, 1, b]]], 1)
         return jnp.dot(picked, tof[j, b], preferred_element_type=jnp.float32)
 
     sums[terms] = jnp.zeros((16, 128), jnp.float32)
+    measured_load.wait()
 
     for t in range(time_blocks):
         span = slice(t * 128, (t + 1) * 128)
@@ -172,41 +170,94 @@
 
     pl.semaphore_wait(barrier, greeted)
 
-    def adjoint_sends(it, first):
-        def send_stop(i, carry):
-            j = far_first(i)
-            if first:
-                pltpu.make_async_copy(tof_hbm.at[j], tof.at[j], load_sem.at[j]).wait()
-            for b in range(blocks):
-                partials_out[it, j, b] = adjoint_block(j, b).astype(jnp.bfloat16)
+    def each_block(work):
+        def some(i, carry):
+            for k in range(UNROLL):
+                work(i * UNROLL + k)
+            return carry
+
+        lax.fori_loop(0, blocks // UNROLL, some, 0)
+
+    def adjoint_stop(it, j, first):
+        if first:
+            loads[j].wait()
+
+        def work(b):
+            value = adjoint_block(j, b)
+            if j == HALF:
+                total[b] = value
+            elif j in (2, 6):
+                relay[j // 4, b] = value
+            else:
+                part_out[it, j, b] = value.astype(jnp.bfloat16)
+
+        each_block(work)
+        if j not in (HALF, 2, 6):
             part_copy(it, j).start()
-            return carry
-
-        lax.fori_loop(0, STOPS - 1, send_stop, 0)
-        if first:
-            loads[HALF].wait()
-        for b in range(blocks):
-            total[b] = adjoint_block(HALF, b)
-
-    def adjoint_gather(it):
-        def add_stop(i, carry):
-            j = near_first(i)
+
+    def adjoint_relay(it, j):
+        arrivals = (0, 1) if j == 2 else (7,)
+        for k in arrivals:
+            part_copy(it, k).wait_recv()
+        for b in range(blocks):
+            value = relay[j // 4, b]
+            for k in arrivals:
+                value = value + part_in[it, k, b].astype(jnp.float32)
+            part_out[it, j, b] = value.astype(jnp.bfloat16)
+        part_copy(it, j).start()
+
+    def back_block(it, b):
+        value = total[b]
+        for j in (3, 5, 6, 2):
+            value = value + part_in[it, j, b].astype(jnp.float32)
+        return value
+
+    def arrived(it):
+        for j in (3, 5, 6, 2):
             part_copy(it, j).wait_recv()
-            for b in range(blocks):
-                total[b] = total[b] + partials_in[it, j, b].astype(jnp.float32)
-            return carry
-
-        lax.fori_loop(0, STOPS - 1, add_stop, 0)
+
+    def forward_stop(it, j):
+        start = MET.index(j) * 2 * blocks
+        each_block(lambda b: forward_block(it, j, b, start + b))
+        for place in range(start + blocks, start + 2 * blocks):
+            sums[place] = sums[place] + sums[prev_ref[0, place]]
+
+    index_copies = [
+        pltpu.make_async_copy(prev_block, prev_ref, index_sem.at[0]),
+        pltpu.make_async_copy(last_block, last_ref, index_sem.at[1]),
+        pltpu.make_async_copy(inverse_block, inverse_ref, index_sem.at[2]),
+    ]
+
+    def index_terms():
+        flat = jnp.concatenate([rows_block[j, k : k + 1, :] for j in MET for k in range(2)], 1)
+        shape = (time_blocks, terms)
+        same = flat == lax.broadcasted_iota(jnp.int32, shape, 0)
+        place = lax.broadcasted_iota(jnp.int32, shape, 1)
+        seen = jnp.where(same, place, -1)
+        span = 1
+        while span < terms:
+            moved = jnp.where(place >= span, pltpu.roll(seen, span, 1), -1)
+            seen = jnp.maximum(seen, moved)
+            span *= 2
+        before = jnp.where(place >= 1, pltpu.roll(seen, 1, 1), -1)
+        prev = jnp.max(jnp.where(same, before, -1), 0, keepdims=True)
+        prev_block[...] = jnp.where(prev < 0, terms, prev)
+        last = jnp.max(seen, 1, keepdims=True)
+        last_block[...] = jnp.broadcast_to(jnp.where(last < 0, terms, last), last_block.shape)
+        shape = (sectors, sectors)
+        owned = owner_block[...] == lax.broadcasted_iota(jnp.int32, shape, 0)
+        inverse = jnp.max(
+            jnp.where(owned, lax.broadcasted_iota(jnp.int32, shape, 1), 0), 1, keepdims=True
+        )
+        inverse_block[...] = jnp.broadcast_to(inverse, inverse_block.shape)
+        for copy in index_copies:
+            copy.start()
 
     def publish(it):
         for b in range(blocks):
             shares[it, HALF, b] = xbar[b].astype(jnp.bfloat16)
-
-        def send(i, carry):
-            share_copy(it, far_first(i)).start()
-            return carry
-
-        lax.fori_loop(0, STOPS - 1, send, 0)
+        for j in (2, 6, 3, 5):
+            share_copy(it, j).start()
         for b in range(blocks):
             edge_out[it, 0, pl.ds(b, 1)] = xbar[b, 0:1]
             edge_out[it, 1, pl.ds(b, 1)] = xbar[b, 15:16]
@@ -219,7 +270,7 @@
                 rolled[a * blocks + b] = pltpu.roll(value, 32 * a, 1)
 
         def gather_band(k, carry):
-            j = inverse_ref[k]
+            j = inverse_ref[k, 0]
             block, lane = j // 4, lax.rem(j, 4)
             parts = [
                 rolled[lax.rem(r - lane + 4, 4) * blocks + block, 4 * r : 4 * r + 4]
@@ -290,10 +341,16 @@
             out.append(jnp.where(quarter < 2, low, high))
         return out
 
-    adjoint_sends(0, True)
-    adjoint_gather(0)
+    for j in SENT:
+        adjoint_stop(0, j, True)
+    index_terms()
+    adjoint_relay(0, 6)
+    adjoint_relay(0, 2)
+    for copy in index_copies:
+        copy.wait()
+    arrived(0)
     for b in range(blocks):
-        image = jnp.maximum(0.0 - primal_step * total[b], 0.0)
+        image = jnp.maximum(0.0 - primal_step * back_block(0, b), 0.0)
         image_ref[:, b * 128 : (b + 1) * 128] = image
         xbar[b] = 2.0 * image
         depth[b] = jnp.zeros((16, 128), jnp.float32)
@@ -302,39 +359,43 @@
 
     def iteration(it, carry):
         publish(it)
-        forward_stop(it, HALF, 0)
-
-        def early(i, carry):
-            j = near_first(i)
+        forward_stop(it, HALF)
+        share_copy(it, 2).wait_recv()
+        share_copy(it, 0).start()
+        share_copy(it, 1).start()
+        share_copy(it, 6).wait_recv()
+        share_copy(it, 7).start()
+        second_hop(it, 0, bands, tiles)
+        forward_stop(it, 2)
+        forward_stop(it, 6)
+        for j in (3, 5, 1, 7, 0):
             share_copy(it, j).wait_recv()
-            forward_stop(it, j, i + 1)
-            return carry
-
-        lax.fori_loop(0, 3, early, 0)
-        second_hop(it, 0, bands, tiles)
-        lax.fori_loop(3, STOPS - 1, early, 0)
+            forward_stop(it, j)
         for t in range(time_blocks):
             span = slice(t * 128, (t + 1) * 128)
-            moved = sums[prev_ref[terms + t]] - measured_ref[:, span]
+            moved = sums[last_ref[t, 0]] - measured_ref[:, span]
             dual = (data_ref[:, span] + dual_step * moved) / (1.0 + dual_step)
             data_ref[:, span] = dual
             dual_half[t] = dual.astype(jnp.bfloat16)
-        adjoint_sends(it + 1, False)
+        for j in SENT:
+            adjoint_stop(it + 1, j, False)
         finish_hops(it, 0, tiles)
         update_wave(it)
         first_hop(it, 1, back_bands)
         update_depth(it)
+        adjoint_relay(it + 1, 6)
+        adjoint_relay(it + 1, 2)
         second_hop(it, 1, back_bands, wave_back)
-        adjoint_gather(it + 1)
         finish_hops(it, 1, wave_back)
         spread_bands(lambda g: wave_back[it, g], sectors)
         for b in range(blocks):
             for r, part in enumerate(joined_bands(lambda j: owner_ref[j], b)):
                 total[b, 4 * r : 4 * r + 4] = total[b, 4 * r : 4 * r + 4] + part
+        arrived(it + 1)
         for b in range(blocks):
             span = slice(b * 128, (b + 1) * 128)
             shifted = jnp.where(row_ids == 0, halo[b : b + 1], pltpu.roll(depth[b], 1, 0))
-            update = total[b] + (shifted - depth[b])
+            update = back_block(it + 1, b) + (shifted - depth[b])
             old = image_ref[:, span]
             image = jnp.maximum(old - primal_step * update, 0.0)
             xbar[b] = 2.0 * image - old
@@ -348,15 +409,12 @@
         for r, part in enumerate(joined_bands(lambda j: j, b)):
             wave_ref[4 * r : 4 * r + 4, b * 128 : (b + 1) * 128] = part
 
-    def drain(i, carry):
-        j = far_first(i)
-        for it in range(ITERS):
-            part_copy(it, j).wait_send()
-        for it in range(ITERS - 1):
-            share_copy(it, j).wait_send()
-        return carry
-
-    lax.fori_loop(0, STOPS - 1, drain, 0)
+    for j in range(STOPS):
+        if j != HALF:
+            for it in range(ITERS - 1):
+                share_copy(it, j).wait_send()
+            for it in range(ITERS):
+                part_copy(it, j).wait_send()
     for it in range(ITERS - 1):
         edge_copy(it, 0).wait_send()
         edge_copy(it, 1).wait_send()
@@ -376,20 +434,10 @@
     slabs = lax.axis_size("slab")
     groups = sectors // ZS
     terms = stops * blocks * slots
-    met = [HALF] + [far_first(i) for i in range(STOPS - 2, -1, -1)]
-    rows = jnp.concatenate([tof_rows[j].reshape(-1) for j in met])
-    order = jnp.arange(terms, dtype=jnp.int32)
-    wanted = jnp.concatenate([rows, jnp.arange(time_blocks, dtype=jnp.int32)])
-    limit = jnp.concatenate([order, jnp.full((time_blocks,), terms, jnp.int32)])
-    match = jnp.logical_and(rows[None] == wanted[:, None], order[None] < limit[:, None])
-    prev = jnp.max(jnp.where(match, order[None], -1), 1)
-    prev = jnp.where(prev < 0, terms, prev)
-    bands = jnp.arange(sectors, dtype=jnp.int32)
-    inverse = jnp.sum(jnp.where(tile_owner[None] == bands[:, None], bands[None], 0), 1)
-
+    rows = tof_rows.transpose(0, 2, 1)
     vmem = pl.BlockSpec(memory_space=pltpu.VMEM)
     smem = pl.BlockSpec(memory_space=pltpu.SMEM)
-    f32, half = jnp.float32, jnp.bfloat16
+    f32, half, i32 = jnp.float32, jnp.bfloat16, jnp.int32
     field = (blocks, depth_rows, width)
     again = ITERS - 1
     ring = (groups, ZS, depth_rows // 4, width)
@@ -400,10 +448,17 @@
             jax.ShapeDtypeStruct(measured.shape, f32),
             jax.ShapeDtypeStruct((depth_rows, pixels), f32),
         ),
-        in_specs=[smem] * 4 + [vmem, pl.BlockSpec(memory_space=pl.ANY)],
+        in_specs=[smem, smem, vmem, vmem] + [pl.BlockSpec(memory_space=pl.ANY)] * 2,
         out_specs=(vmem, vmem, vmem),
         scratch_shapes=[
             pltpu.VMEM((stops, blocks, slots * width, width), half),
+            pltpu.VMEM(measured.shape, f32),
+            pltpu.VMEM((1, terms), i32),
+            pltpu.VMEM((time_blocks, width), i32),
+            pltpu.VMEM((sectors, width), i32),
+            pltpu.SMEM((1, terms), i32),
+            pltpu.SMEM((time_blocks, width), i32),
+            pltpu.SMEM((sectors, width), i32),
             pltpu.VMEM((terms + 1, depth_rows, width), f32),
             pltpu.VMEM((time_blocks, depth_rows, width), half),
             pltpu.VMEM(field, f32),
@@ -413,6 +468,7 @@
             pltpu.VMEM((again, stops) + field, half),
             pltpu.VMEM((ITERS, stops) + field, half),
             pltpu.VMEM((ITERS, stops) + field, half),
+            pltpu.VMEM((2,) + field, f32),
             pltpu.VMEM((again, 2, blocks, width), f32),
             pltpu.VMEM((again, 2, blocks, width), f32),
             pltpu.VMEM((4 * blocks, depth_rows, width), f32),
@@ -423,7 +479,8 @@
             pltpu.VMEM((4, sectors, depth_rows // 4, width), f32),
             pltpu.VMEM((again,) + ring, f32),
             pltpu.VMEM((again,) + ring, f32),
-            pltpu.SemaphoreType.DMA((stops,)),
+            pltpu.SemaphoreType.DMA((stops + 1,)),
+            pltpu.SemaphoreType.DMA((3,)),
             pltpu.SemaphoreType.DMA((again, stops)),
             pltpu.SemaphoreType.DMA((again, stops)),
             pltpu.SemaphoreType.DMA((ITERS, stops)),
@@ -434,9 +491,9 @@
             pltpu.SemaphoreType.DMA((again, 2, 2, ZS)),
         ],
         compiler_params=pltpu.CompilerParams(
-            collective_id=0, has_side_effects=True, vmem_limit_bytes=48 * 1024 * 1024
+            collective_id=0, has_side_effects=True, vmem_limit_bytes=60 * 1024 * 1024
         ),
-    )(tof_rows.reshape(-1), prev, tile_owner, inverse, measured, tof.reshape(stops, blocks, slots * width, width))
+    )(rows, tile_owner, rows, tile_owner[None], measured, tof.reshape(stops, blocks, slots * width, width))
 
 
 def solution(mesh):

time: 122 us -> 94.3 us (0.77)
  Pallas kernels: 111 us -> 88.2 us
  local copies, waits for them, and re-layouts: 6.92 us -> 4.81 us
  other arithmetic: 1.69 us -> 0 us
    pallas_call x1, Pallas kernels: 111 us -> 88.2 us  [body(): pl.pallas_call(functools.partial(kernel, sectors, groups, slabs, blocks,...]
    slice x9 -> x0, local copies, waits for them, and re-layouts: 1.47 us -> none  [body(): rows = jnp.concatenate([tof_rows[j].reshape(-1) for j in met])]
    unnamed x8 -> x3, local copies, waits for them, and re-layouts: 4.43 us -> 4.81 us
where the time goes in v3:
time: 94.3 us; the launch traced here: 93.7 us
  Pallas kernels  88.2 us (94%)
  local copies, waits for them, and re-layouts  4.81 us (5%)
    pallas_call x1, Pallas kernels, body(): pl.pallas_call(functools.partial(kernel, sectors, groups, slabs, blocks,...  88.2 us
    unnamed x3, local copies, waits for them, and re-layouts  4.81 us

profile of v3, /device:TPU:8, one launch (start us, length us, event | category | flops | bytes accessed | tf_op | source)
XLA Modules:
  0.0 93.7 jit_solution(850930545364910827)
XLA Ops:
  0.6 88.2 %shard_map.67 = (f32[16,2048]{1,0:T(8,128)}, f32[16,4096]{1,0:T(8,128)}, f32[16,2048]{1,0:T(8,128)}) custom-call(s32[8,2,16]{2,1,0:T(2,128)} %bitcast.4, s32[64]{0:T(128)} %owner_ref.1, s32[8,2,16]{2,1,0:T(2,128)} %bitcast.5, s32[1,64]{1,0:T(1,128)} %bitcast.6, f32[16,4096]{1,0:T(8,128)} %measured_hbm.1, bf16[8,16,256,128]{3,2,1,0:T(8,128)(2,1)} %bitcast.3), custom_call_target="tpu_custom_call" | custom-call | tf_op jit(solution)/shard_map/pallas_call | solution.py:444
  88.9 1.6 %copy.10 = f32[16,2048]{1,0:T(8,128)} copy(f32[16,2048]{1,0:T(8,128)} %get-tuple-element.6) | data formatting | bytes 262144
  90.4 1.7 %copy.11 = f32[16,4096]{1,0:T(8,128)} copy(f32[16,4096]{1,0:T(8,128)} %get-tuple-element.7) | data formatting | bytes 524288
  92.1 1.6 %copy.12 = f32[16,2048]{1,0:T(8,128)} copy(f32[16,2048]{1,0:T(8,128)} %get-tuple-element.8) | data formatting | bytes 262144

commit v4 on v3

--- a/solution.py
+++ b/solution.py
@@ -21,7 +21,7 @@
 MET = (4, 2, 6, 3, 5, 1, 7, 0)
 SENT = (0, 1, 7, 3, 5, 2, 6, 4)
 HOPS = {0: -2, 1: -1, 7: 1, 3: -1, 5: 1, 2: -2, 6: 2}
-UNROLL = 8
+UNROLL = 16
 
 
 def kernel(
@@ -368,7 +368,14 @@
         second_hop(it, 0, bands, tiles)
         forward_stop(it, 2)
         forward_stop(it, 6)
-        for j in (3, 5, 1, 7, 0):
+        for j in (3, 5):
+            share_copy(it, j).wait_recv()
+            forward_stop(it, j)
+        finish_hops(it, 0, tiles)
+        update_wave(it)
+        first_hop(it, 1, back_bands)
+        update_depth(it)
+        for j in (1, 7, 0):
             share_copy(it, j).wait_recv()
             forward_stop(it, j)
         for t in range(time_blocks):
@@ -379,13 +386,9 @@
             dual_half[t] = dual.astype(jnp.bfloat16)
         for j in SENT:
             adjoint_stop(it + 1, j, False)
-        finish_hops(it, 0, tiles)
-        update_wave(it)
-        first_hop(it, 1, back_bands)
-        update_depth(it)
+        second_hop(it, 1, back_bands, wave_back)
         adjoint_relay(it + 1, 6)
         adjoint_relay(it + 1, 2)
-        second_hop(it, 1, back_bands, wave_back)
         finish_hops(it, 1, wave_back)
         spread_bands(lambda g: wave_back[it, g], sectors)
         for b in range(blocks):
@@ -423,6 +426,19 @@
                 zed_copy(it, way, source, offset).wait_send()
             for offset in range(1, groups):
                 group_copy(it, way, dest, offset).wait_send()
+
+
+def deliver(a, b, c, a_out, b_out, c_out, a_held, b_held, c_held, sem):
+    ways = ((a, a_held, a_out), (b, b_held, b_out), (c, c_held, c_out))
+    loads = [pltpu.make_async_copy(w[0], w[1], sem.at[0, i]) for i, w in enumerate(ways)]
+    stores = [pltpu.make_async_copy(w[1], w[2], sem.at[1, i]) for i, w in enumerate(ways)]
+    for load in loads:
+        load.start()
+    for load, store in zip(loads, stores):
+        load.wait()
+        store.start()
+    for store in stores:
+        store.wait()
 
 
 def body(measured, tof, tof_rows, tile_owner):
@@ -441,7 +457,7 @@
     field = (blocks, depth_rows, width)
     again = ITERS - 1
     ring = (groups, ZS, depth_rows // 4, width)
-    return pl.pallas_call(
+    results = pl.pallas_call(
         functools.partial(kernel, sectors, groups, slabs, blocks, time_blocks),
         out_shape=(
             jax.ShapeDtypeStruct((depth_rows, pixels), f32),
@@ -494,6 +510,15 @@
             collective_id=0, has_side_effects=True, vmem_limit_bytes=60 * 1024 * 1024
         ),
     )(rows, tile_owner, rows, tile_owner[None], measured, tof.reshape(stops, blocks, slots * width, width))
+    anywhere = pl.BlockSpec(memory_space=pl.ANY)
+    return pl.pallas_call(
+        deliver,
+        out_shape=tuple(jax.ShapeDtypeStruct(r.shape, r.dtype) for r in results),
+        in_specs=[anywhere] * 3,
+        out_specs=(anywhere,) * 3,
+        scratch_shapes=[pltpu.VMEM(r.shape, r.dtype) for r in results]
+        + [pltpu.SemaphoreType.DMA((2, 3))],
+    )(*results)
 
 
 def solution(mesh):

time: 94.3 us -> 88.9 us (0.943)
  the two profiles are of different devices: /device:TPU:8 before, /device:TPU:64 now
where the time goes in v4:
time: 88.9 us; the launch traced here: 88.7 us
  Pallas kernels  88.1 us (99%)
    pallas_call x1, Pallas kernels, body(): pl.pallas_call(functools.partial(kernel, sectors, groups, slabs, blocks,...  86.3 us
    pallas_call x1, Pallas kernels, body(): pl.pallas_call(deliver, out_shape=tuple((jax.ShapeDtypeStruct(r.shape, r....  1.81 us

profile of v4, /device:TPU:64, one launch (start us, length us, event | category | flops | bytes accessed | tf_op | source)
XLA Modules:
  0.0 88.7 jit_solution(5170657900100476615)
XLA Ops:
  0.6 86.3 %shard_map.67 = (f32[16,2048]{1,0:T(8,128)}, f32[16,4096]{1,0:T(8,128)}, f32[16,2048]{1,0:T(8,128)}) custom-call(s32[8,2,16]{2,1,0:T(2,128)} %bitcast.4, s32[64]{0:T(128)} %owner_ref.1, s32[8,2,16]{2,1,0:T(2,128)} %bitcast.5, s32[1,64]{1,0:T(1,128)} %bitcast.6, f32[16,4096]{1,0:T(8,128)} %measured_hbm.1, bf16[8,16,256,128]{3,2,1,0:T(8,128)(2,1)} %bitcast.3), custom_call_target="tpu_custom_call" | custom-call | tf_op jit(solution)/shard_map/pallas_call | solution.py:460
  86.9 1.8 %shard_map.68 = (f32[16,2048]{1,0:T(8,128)}, f32[16,4096]{1,0:T(8,128)}, f32[16,2048]{1,0:T(8,128)}) custom-call(f32[16,2048]{1,0:T(8,128)} %get-tuple-element.6.a, f32[16,4096]{1,0:T(8,128)} %get-tuple-element.7.b, f32[16,2048]{1,0:T(8,128)} %get-tuple-element.8.c), custom_call_target="tpu_custom_call" | custom-call | tf_op jit(solution)/shard_map/pallas_call | solution.py:514

commit v5 on v4

--- a/solution.py
+++ b/solution.py
@@ -30,7 +30,7 @@
     image_ref, data_ref, wave_ref,
     tof, measured_ref, prev_block, last_block, inverse_block, prev_ref, last_ref, inverse_ref, sums, dual_half, xbar, depth, halo, total,
     shares, part_out, part_in, relay, edge_out, edge_in,
-    rolled, bands, mid, tiles, wave, rolled_back, back_bands, wave_back,
+    rolled, bands, turned, zed_out, zed_in, group_out, group_in, wave, rolled_back,
     load_sem, index_sem, share_send, share_recv, part_send, part_recv, edge_send, edge_recv,
     band_send, band_recv,
 ):
@@ -44,7 +44,7 @@
     ]
     measured_load = pltpu.make_async_copy(measured_hbm, measured_ref, load_sem.at[STOPS])
     measured_load.start()
-    for j in SENT:
+    for j in SENT[:3]:
         loads[j].start()
 
     def sector_at(offset):
@@ -103,49 +103,69 @@
             device_id={"slab": slab_at(1 if way else -1)},
         )
 
-    def zed_copy(it, way, source, offset):
+    def zed_copy(it, way, offset):
         return pltpu.make_async_remote_copy(
-            src_ref=source.at[it, :, zed_at(offset)], dst_ref=mid.at[it, way, :, zed],
+            src_ref=zed_out.at[it, way, zed_at(offset)], dst_ref=zed_in.at[it, way, zed],
             send_sem=band_send.at[it, way, 0, offset], recv_sem=band_recv.at[it, way, 0, offset],
             device_id={"sector": group * ZS + zed_at(offset)},
         )
 
-    def zed_wait(it, way, source, offset):
+    def zed_wait(it, way, offset):
         pltpu.make_async_remote_copy(
-            src_ref=source.at[it, :, zed_at(offset)], dst_ref=mid.at[it, way, :, zed_at(ZS - offset)],
+            src_ref=zed_out.at[it, way, zed_at(offset)], dst_ref=zed_in.at[it, way, zed_at(ZS - offset)],
             send_sem=band_send.at[it, way, 0, offset], recv_sem=band_recv.at[it, way, 0, offset],
             device_id={"sector": group * ZS + zed_at(offset)},
         ).wait_recv()
 
-    def group_copy(it, way, dest, offset):
+    def group_copy(it, way, offset):
         return pltpu.make_async_remote_copy(
-            src_ref=mid.at[it, way, group_at(offset)], dst_ref=dest.at[it, group],
+            src_ref=group_out.at[it, way, group_at(offset)], dst_ref=group_in.at[it, way, group],
             send_sem=band_send.at[it, way, 1, offset], recv_sem=band_recv.at[it, way, 1, offset],
             device_id={"sector": group_at(offset) * ZS + zed},
         )
 
-    def group_wait(it, way, dest, offset):
+    def group_wait(it, way, offset):
         pltpu.make_async_remote_copy(
-            src_ref=mid.at[it, way, group_at(offset)], dst_ref=dest.at[it, group_at(groups - offset)],
+            src_ref=group_out.at[it, way, group_at(offset)],
+            dst_ref=group_in.at[it, way, group_at(groups - offset)],
             send_sem=band_send.at[it, way, 1, offset], recv_sem=band_recv.at[it, way, 1, offset],
             device_id={"sector": group_at(offset) * ZS + zed},
         ).wait_recv()
 
-    def first_hop(it, way, source):
+    def joined(pieces):
+        return jnp.concatenate(pieces, 0).astype(jnp.bfloat16)
+
+    def first_hop(it, way):
+        for z in range(ZS):
+            for q in range(groups // 4):
+                zed_out[it, way, z, q] = joined([bands[4 * q + i, z] for i in range(4)])
         for offset in range(1, ZS):
-            zed_copy(it, way, source, offset).start()
-        mid[it, way, :, pl.ds(zed, 1)] = source[it, :, pl.ds(zed, 1)]
-
-    def second_hop(it, way, source, dest):
+            zed_copy(it, way, offset).start()
+        zed_in[it, way, pl.ds(zed, 1)] = zed_out[it, way, pl.ds(zed, 1)]
+
+    def second_hop(it, way):
         for offset in range(1, ZS):
-            zed_wait(it, way, source, offset)
+            zed_wait(it, way, offset)
+        for z in range(ZS):
+            for q in range(groups // 4):
+                value = zed_in[it, way, z, q].astype(jnp.float32)
+                for i in range(4):
+                    turned[4 * q + i, z] = value[4 * i : 4 * i + 4]
+        for g in range(groups):
+            for q in range(ZS // 4):
+                group_out[it, way, g, q] = joined([turned[g, 4 * q + i] for i in range(4)])
         for offset in range(1, groups):
-            group_copy(it, way, dest, offset).start()
-        dest[it, pl.ds(group, 1)] = mid[it, way, pl.ds(group, 1)]
-
-    def finish_hops(it, way, dest):
+            group_copy(it, way, offset).start()
+        group_in[it, way, pl.ds(group, 1)] = group_out[it, way, pl.ds(group, 1)]
+
+    def finish_hops(it, way):
         for offset in range(1, groups):
-            group_wait(it, way, dest, offset)
+            group_wait(it, way, offset)
+        for g in range(groups):
+            for q in range(ZS // 4):
+                value = group_in[it, way, g, q].astype(jnp.float32)
+                for i in range(4):
+                    bands[g, 4 * q + i] = value[4 * i : 4 * i + 4]
 
     def forward_block(it, j, b, place):
         out = lax.dot_general(
@@ -168,6 +188,8 @@
         data_ref[:, span] = dual
         dual_half[t] = dual.astype(jnp.bfloat16)
 
+    for j in SENT[3:]:
+        loads[j].start()
     pl.semaphore_wait(barrier, greeted)
 
     def each_block(work):
@@ -278,11 +300,11 @@
             ]
             low = jnp.where(quarter == 0, parts[0], parts[1])
             high = jnp.where(quarter == 2, parts[2], parts[3])
-            bands[it, k // ZS, lax.rem(k, ZS)] = jnp.where(quarter < 2, low, high)
+            bands[k // ZS, lax.rem(k, ZS)] = jnp.where(quarter < 2, low, high)
             return carry
 
         lax.fori_loop(0, sectors, gather_band, 0, unroll=8)
-        first_hop(it, 0, bands)
+        first_hop(it, 0)
 
     def haar(upper, lower):
         def pairs(value):
@@ -295,7 +317,7 @@
 
     def update_wave(it):
         for g in range(groups):
-            full = tiles[it, g]
+            full = bands[g]
             upper = jnp.concatenate([full[2 * (i // 2)][None] for i in range(ZS)], 0)
             lower = jnp.concatenate([full[2 * (i // 2) + 1][None] for i in range(ZS)], 0)
             odd = lax.rem(lax.broadcasted_iota(jnp.int32, (ZS, 4, 128), 0), 2) == 1
@@ -307,7 +329,7 @@
             upper = jnp.concatenate([dual[2 * (i // 2)][None] for i in range(ZS)], 0)
             lower = jnp.concatenate([dual[2 * (i // 2) + 1][None] for i in range(ZS)], 0)
             top, low = haar(upper, lower)
-            back_bands[it, g] = jnp.where(odd, low, top)
+            bands[g] = jnp.where(odd, low, top)
 
     def update_depth(it):
         edge_copy(it, 0).wait_recv()
@@ -365,15 +387,15 @@
         share_copy(it, 1).start()
         share_copy(it, 6).wait_recv()
         share_copy(it, 7).start()
-        second_hop(it, 0, bands, tiles)
+        second_hop(it, 0)
         forward_stop(it, 2)
         forward_stop(it, 6)
         for j in (3, 5):
             share_copy(it, j).wait_recv()
             forward_stop(it, j)
-        finish_hops(it, 0, tiles)
+        finish_hops(it, 0)
         update_wave(it)
-        first_hop(it, 1, back_bands)
+        first_hop(it, 1)
         update_depth(it)
         for j in (1, 7, 0):
             share_copy(it, j).wait_recv()
@@ -386,11 +408,15 @@
             dual_half[t] = dual.astype(jnp.bfloat16)
         for j in SENT:
             adjoint_stop(it + 1, j, False)
-        second_hop(it, 1, back_bands, wave_back)
+        second_hop(it, 1)
         adjoint_relay(it + 1, 6)
         adjoint_relay(it + 1, 2)
-        finish_hops(it, 1, wave_back)
-        spread_bands(lambda g: wave_back[it, g], sectors)
+        spread_bands(lambda g: wave[g], sectors)
+        for b in range(blocks):
+            for r, part in enumerate(joined_bands(lambda j: j, b)):
+                wave_ref[4 * r : 4 * r + 4, b * 128 : (b + 1) * 128] = part
+        finish_hops(it, 1)
+        spread_bands(lambda g: bands[g], sectors)
         for b in range(blocks):
             for r, part in enumerate(joined_bands(lambda j: owner_ref[j], b)):
                 total[b, 4 * r : 4 * r + 4] = total[b, 4 * r : 4 * r + 4] + part
@@ -406,11 +432,6 @@
         return carry
 
     lax.fori_loop(0, ITERS - 1, iteration, 0)
-
-    spread_bands(lambda g: wave[g], sectors)
-    for b in range(blocks):
-        for r, part in enumerate(joined_bands(lambda j: j, b)):
-            wave_ref[4 * r : 4 * r + 4, b * 128 : (b + 1) * 128] = part
 
     for j in range(STOPS):
         if j != HALF:
@@ -421,11 +442,11 @@
     for it in range(ITERS - 1):
         edge_copy(it, 0).wait_send()
         edge_copy(it, 1).wait_send()
-        for way, source, dest in ((0, bands, tiles), (1, back_bands, wave_back)):
+        for way in range(2):
             for offset in range(1, ZS):
-                zed_copy(it, way, source, offset).wait_send()
+                zed_copy(it, way, offset).wait_send()
             for offset in range(1, groups):
-                group_copy(it, way, dest, offset).wait_send()
+                group_copy(it, way, offset).wait_send()
 
 
 def deliver(a, b, c, a_out, b_out, c_out, a_held, b_held, c_held, sem):
@@ -488,13 +509,14 @@
             pltpu.VMEM((again, 2, blocks, width), f32),
             pltpu.VMEM((again, 2, blocks, width), f32),
             pltpu.VMEM((4 * blocks, depth_rows, width), f32),
-            pltpu.VMEM((again,) + ring, f32),
-            pltpu.VMEM((again, 2) + ring, f32),
-            pltpu.VMEM((again,) + ring, f32),
+            pltpu.VMEM(ring, f32),
+            pltpu.VMEM(ring, f32),
+            pltpu.VMEM((again, 2, ZS, groups // 4, 16, width), half),
+            pltpu.VMEM((again, 2, ZS, groups // 4, 16, width), half),
+            pltpu.VMEM((again, 2, groups, ZS // 4, 16, width), half),
+            pltpu.VMEM((again, 2, groups, ZS // 4, 16, width), half),
             pltpu.VMEM(ring, f32),
             pltpu.VMEM((4, sectors, depth_rows // 4, width), f32),
-            pltpu.VMEM((again,) + ring, f32),
-            pltpu.VMEM((again,) + ring, f32),
             pltpu.SemaphoreType.DMA((stops + 1,)),
             pltpu.SemaphoreType.DMA((3,)),
             pltpu.SemaphoreType.DMA((again, stops)),

time: 88.9 us -> 85.8 us (0.965)
  the two profiles are of different devices: /device:TPU:64 before, /device:TPU:8 now
where the time goes in v5:
time: 85.8 us; the launch traced here: 85 us
  Pallas kernels  84.4 us (98%)
    pallas_call x1, Pallas kernels, body(): pl.pallas_call(functools.partial(kernel, sectors, groups, slabs, blocks,...  82.6 us
    pallas_call x1, Pallas kernels, body(): pl.pallas_call(deliver, out_shape=tuple((jax.ShapeDtypeStruct(r.shape, r....  1.81 us

profile of v5, /device:TPU:8, one launch (start us, length us, event | category | flops | bytes accessed | tf_op | source)
XLA Modules:
  0.0 85.0 jit_solution(8086848974732256552)
XLA Ops:
  0.6 82.6 %shard_map.67 = (f32[16,2048]{1,0:T(8,128)}, f32[16,4096]{1,0:T(8,128)}, f32[16,2048]{1,0:T(8,128)}) custom-call(s32[8,2,16]{2,1,0:T(2,128)} %bitcast.4, s32[64]{0:T(128)} %owner_ref.1, s32[8,2,16]{2,1,0:T(2,128)} %bitcast.5, s32[1,64]{1,0:T(1,128)} %bitcast.6, f32[16,4096]{1,0:T(8,128)} %measured_hbm.1, bf16[8,16,256,128]{3,2,1,0:T(8,128)(2,1)} %bitcast.3), custom_call_target="tpu_custom_call" | custom-call | tf_op jit(solution)/shard_map/pallas_call | solution.py:481
  83.2 1.8 %shard_map.68 = (f32[16,2048]{1,0:T(8,128)}, f32[16,4096]{1,0:T(8,128)}, f32[16,2048]{1,0:T(8,128)}) custom-call(f32[16,2048]{1,0:T(8,128)} %get-tuple-element.6.a, f32[16,4096]{1,0:T(8,128)} %get-tuple-element.7.b, f32[16,2048]{1,0:T(8,128)} %get-tuple-element.8.c), custom_call_target="tpu_custom_call" | custom-call | tf_op jit(solution)/shard_map/pallas_call | solution.py:536

commit v6 on v5

--- a/solution.py
+++ b/solution.py
@@ -393,11 +393,13 @@
         for j in (3, 5):
             share_copy(it, j).wait_recv()
             forward_stop(it, j)
+        share_copy(it, 1).wait_recv()
+        forward_stop(it, 1)
         finish_hops(it, 0)
         update_wave(it)
         first_hop(it, 1)
         update_depth(it)
-        for j in (1, 7, 0):
+        for j in (7, 0):
             share_copy(it, j).wait_recv()
             forward_stop(it, j)
         for t in range(time_blocks):

time: 85.8 us -> 86.1 us (level)
  no operation moved by 1% of the time
where the time goes in v6:
time: 86.1 us; the launch traced here: 85.8 us
  Pallas kernels  85.2 us (99%)
    pallas_call x1, Pallas kernels, body(): pl.pallas_call(functools.partial(kernel, sectors, groups, slabs, blocks,...  83.4 us
    pallas_call x1, Pallas kernels, body(): pl.pallas_call(deliver, out_shape=tuple((jax.ShapeDtypeStruct(r.shape, r....  1.81 us

profile of v6, /device:TPU:8, one launch (start us, length us, event | category | flops | bytes accessed | tf_op | source)
XLA Modules:
  0.0 85.8 jit_solution(16775747152728431532)
XLA Ops:
  0.6 83.4 %shard_map.67 = (f32[16,2048]{1,0:T(8,128)}, f32[16,4096]{1,0:T(8,128)}, f32[16,2048]{1,0:T(8,128)}) custom-call(s32[8,2,16]{2,1,0:T(2,128)} %bitcast.4, s32[64]{0:T(128)} %owner_ref.1, s32[8,2,16]{2,1,0:T(2,128)} %bitcast.5, s32[1,64]{1,0:T(1,128)} %bitcast.6, f32[16,4096]{1,0:T(8,128)} %measured_hbm.1, bf16[8,16,256,128]{3,2,1,0:T(8,128)(2,1)} %bitcast.3), custom_call_target="tpu_custom_call" | custom-call | tf_op jit(solution)/shard_map/pallas_call | solution.py:483
  84.0 1.8 %shard_map.68 = (f32[16,2048]{1,0:T(8,128)}, f32[16,4096]{1,0:T(8,128)}, f32[16,2048]{1,0:T(8,128)}) custom-call(f32[16,2048]{1,0:T(8,128)} %get-tuple-element.6.a, f32[16,4096]{1,0:T(8,128)} %get-tuple-element.7.b, f32[16,2048]{1,0:T(8,128)} %get-tuple-element.8.c), custom_call_target="tpu_custom_call" | custom-call | tf_op jit(solution)/shard_map/pallas_call | solution.py:538
